TPU v7x, 128 devices: a whole 4x4x4 slice. The times are simulated.
128 devices in a mesh: dp: 16 (over y_lo, z, core), tensor: 8 (over x, y_hi).
Axes of the slice: x: 4, y: 4 (y_hi: 2, y_lo: 2; y = y_hi * 2 + y_lo), z: 4, core: 2. Of those that a mesh axis runs over, the one named last changes fastest.
Arguments:
- teacher_queries: bfloat16 [16, 1024, 8192], P('dp', None, 'tensor'), may hold values from -100 to 100
- teacher_keys: bfloat16 [16, 1024, 1024], P('dp', None, 'tensor'), may hold values from -5 to 5
- teacher_values: bfloat16 [16, 1024, 1024], P('dp', None, 'tensor'), may hold values from -6 to 6
- projector: bfloat16 [8192, 4096], P('tensor'), may hold values from -0.25 to 0.25
- student_inputs: bfloat16 [16, 1024, 4096], P('dp', 'tensor'), may hold values from -30 to 30
- query_weight: bfloat16 [4096, 4096], P('dp', 'tensor'), may hold values from -1 to 1
- key_weight: bfloat16 [4096, 1024], P('dp', 'tensor'), may hold values from -1 to 1
- value_weight: bfloat16 [4096, 1024], P('dp', 'tensor'), may hold values from -0.09375 to 0.09375
Outputs:
- query_grad: float32 [4096, 4096], P('dp', 'tensor')
- key_grad: float32 [4096, 1024], P('dp', 'tensor')
- value_grad: float32 [4096, 1024], P('dp', 'tensor')
All inputs are finite; a program needn't handle non-finite values.
Results may differ from a plain program's by a relative error of at most 0.029.
Values may be sent and summed in bfloat16 or wider, within the bound.
No kernel may reach another device: no remote copies, remote signals or barrier semaphores. Data moves between devices by JAX's collectives and lax.ppermute only.
A program may use at most 128 MiB of HBM per device.

v0:
```python
import jax
import jax.numpy as jnp
from jax import lax
from jax.sharding import PartitionSpec as P

HEAD = 128
TQH = 64
TKVH = 8
SQH = 32
SKVH = 8


def attend(queries, keys, values, groups, factor):
    length = queries.shape[0]
    heads_kv = keys.shape[1] // HEAD
    query_heads = queries.reshape(length, heads_kv, groups, HEAD)
    key_heads = keys.reshape(length, heads_kv, HEAD)
    value_heads = values.reshape(length, heads_kv, HEAD)
    block_rows = min(512, length)
    pieces = []
    kept = []
    for number in range(length // block_rows):
        first = number * block_rows
        limit = first + block_rows
        scores = (
            jnp.einsum(
                "qhgd,khd->hgqk",
                query_heads[first:limit],
                key_heads[:limit],
                preferred_element_type=jnp.float32,
            )
            * factor
        )
        visible = jnp.arange(limit)[None, :] <= (first + jnp.arange(block_rows))[:, None]
        scores = jnp.where(visible, scores, -1e30)
        shifted = jnp.exp(scores - jnp.max(scores, axis=-1, keepdims=True))
        probs = shifted / jnp.sum(shifted, axis=-1, keepdims=True)
        rounded = probs.astype(jnp.bfloat16)
        context = jnp.einsum(
            "hgqk,khd->qhgd", rounded, value_heads[:limit], preferred_element_type=jnp.float32
        )
        pieces.append(context.reshape(block_rows, -1))
        kept.append(probs)
    return (jnp.concatenate(pieces, axis=0), kept)


def attend_back(incoming_all, queries, keys, values, kept, groups, factor):
    length = queries.shape[0]
    heads_kv = keys.shape[1] // HEAD
    query_heads = queries.reshape(length, heads_kv, groups, HEAD)
    key_heads = keys.reshape(length, heads_kv, HEAD)
    value_heads = values.reshape(length, heads_kv, HEAD)
    block_rows = min(512, length)
    grad_keys = jnp.zeros((length, heads_kv, HEAD), jnp.float32)
    grad_values = jnp.zeros((length, heads_kv, HEAD), jnp.float32)
    query_parts = []
    for number in range(length // block_rows):
        first = number * block_rows
        limit = first + block_rows
        probs = kept[number]
        rounded = probs.astype(jnp.bfloat16)
        incoming = incoming_all[first:limit].reshape(block_rows, heads_kv, groups, HEAD)
        grad_values = grad_values.at[:limit].add(
            jnp.einsum("hgqk,qhgd->khd", rounded, incoming, preferred_element_type=jnp.float32)
        )
        grad_probs = jnp.einsum(
            "qhgd,khd->hgqk", incoming, value_heads[:limit], preferred_element_type=jnp.float32
        )
        grad_scores = probs * (grad_probs - jnp.sum(grad_probs * probs, axis=-1, keepdims=True))
        scaled = (grad_scores * factor).astype(jnp.bfloat16)
        query_parts.append(
            jnp.einsum(
                "hgqk,khd->qhgd", scaled, key_heads[:limit], preferred_element_type=jnp.float32
            ).reshape(block_rows, -1)
        )
        grad_keys = grad_keys.at[:limit].add(
            jnp.einsum(
                "hgqk,qhgd->khd",
                scaled,
                query_heads[first:limit],
                preferred_element_type=jnp.float32,
            )
        )
    grad_queries = jnp.concatenate(query_parts, axis=0).astype(jnp.bfloat16)
    return (
        grad_queries,
        grad_keys.reshape(length, -1).astype(jnp.bfloat16),
        grad_values.reshape(length, -1).astype(jnp.bfloat16),
    )


def per_device(
    teacher_queries,
    teacher_keys,
    teacher_values,
    projector,
    student_inputs,
    query_weight,
    key_weight,
    value_weight,
):
    factor = HEAD ** (-0.5)
    dp_count = lax.axis_size("dp")
    context_t, unused = attend(
        teacher_queries[0], teacher_keys[0], teacher_values[0], TQH // TKVH, factor
    )
    context_t = context_t.astype(jnp.bfloat16)
    summed = lax.psum_scatter(
        lax.dot_general(
            projector, context_t, (((0,), (1,)), ((), ())), preferred_element_type=jnp.float32
        ).astype(jnp.bfloat16),
        "tensor",
        scatter_dimension=0,
        tiled=True,
    ).astype(jnp.float32)
    target = summed.T
    rows_all = lax.all_gather(student_inputs[0], "tensor", axis=0, tiled=True)
    full_weights = (
        lax.all_gather(query_weight, "dp", axis=0, tiled=True),
        lax.all_gather(key_weight, "dp", axis=0, tiled=True),
        lax.all_gather(value_weight, "dp", axis=0, tiled=True),
    )
    rows_all, full_weights = (rows_all, full_weights)
    queries = jnp.dot(rows_all, full_weights[0], preferred_element_type=jnp.float32).astype(
        jnp.bfloat16
    )
    keys = jnp.dot(rows_all, full_weights[1], preferred_element_type=jnp.float32).astype(
        jnp.bfloat16
    )
    values = jnp.dot(rows_all, full_weights[2], preferred_element_type=jnp.float32).astype(
        jnp.bfloat16
    )
    context_s, kept = attend(queries, keys, values, SQH // SKVH, factor)
    grad_context = ((context_s - target) / dp_count).astype(jnp.bfloat16)
    grad_q, grad_k, grad_v = attend_back(
        grad_context, queries, keys, values, kept, SQH // SKVH, factor
    )
    grad_all = jnp.concatenate([grad_q, grad_k, grad_v], axis=1)
    whole = lax.dot_general(
        rows_all, grad_all, (((0,), (0,)), ((), ())), preferred_element_type=jnp.float32
    )
    reduced = lax.psum_scatter(
        whole.astype(jnp.bfloat16), "dp", scatter_dimension=0, tiled=True
    ).astype(jnp.float32)
    query_cols = query_weight.shape[1]
    key_cols = key_weight.shape[1]
    return (
        reduced[:, :query_cols],
        reduced[:, query_cols : query_cols + key_cols],
        reduced[:, query_cols + key_cols :],
    )


def solution(mesh):
    placed = (
        P("dp", None, "tensor"),
        P("dp", None, "tensor"),
        P("dp", None, "tensor"),
        P("tensor", None),
        P("dp", "tensor", None),
        P("dp", "tensor"),
        P("dp", "tensor"),
        P("dp", "tensor"),
    )
    return jax.shard_map(
        per_device,
        mesh=mesh,
        in_specs=placed,
        out_specs=(P("dp", "tensor"), P("dp", "tensor"), P("dp", "tensor")),
        check_vma=False,
    )
```

profile of v0, /device:TPU:0, one launch (start us, length us, event | category | flops | bytes accessed | tf_op | source)
XLA Modules:
  0.0 461.7 jit_solution(14809512765833337011)
XLA Ops:
  10.1 2.8 fusion.120
  13.9 1.5 copy.95
  15.4 1.5 fusion.23
  16.9 1.8 fusion.18
  20.1 7.4 %fusion.1 = (f32[8,512]{1,0:T(8,128)S(1)}, f32[1024,512,8]{1,0,2:T(8,128)}) fusion(pred[512,1024]{0,1:T(8,128)(4,1)S(1)} %iota_compare_fusion, bf16[512,8,128]{0,2,1:T(8,128)(2,1)S(1)} %bitcast.311, bf16[1,1024,128]{2,1,0:T(8,128)(2,1)S(1)} %copy-done.5), kind=kOutput, calls=%fused_computation.4 | convolution fusion | flops 1086320640 | bytes 18628608 | tf_op jit(solution)/shard_map/qhgd,khd->hgqk/dot_general | solution.py:26
  27.6 9.4 %fusion = f32[8,512]{1,0:T(8,128)S(1)} fusion(f32[1024,512,8]{1,0,2:T(8,128)} %get-tuple-element.86, f32[8,512]{1,0:T(8,128)S(1)} %get-tuple-element.85, pred[512,1024]{0,1:T(8,128)(4,1)S(1)} %iota_compare_fusion), kind=kLoop, calls=%fused_computation.3 | loop fusion | flops 16773120 | bytes 17334272 | tf_op jit(solution)/shard_map/reduce_sum | solution.py:37
  37.0 8.8 %fusion.66 = bf16[8,512,128]{1,2,0:T(8,128)(2,1)S(1)} fusion(f32[8,512]{1,0:T(8,128)S(1)} %fusion, f32[8,512]{1,0:T(8,128)S(1)} %get-tuple-element.85, f32[1024,512,8]{1,0,2:T(8,128)} %get-tuple-element.86, pred[512,1024]{0,1:T(8,128)(4,1)S(1)} %iota_compare_fusion, bf16[1,1024,128]{2,1,0:T(8,128)(2,1)S(1)} %copy-done.10), kind=kOutput, calls=%fused_computation.75 | convolution fusion | flops 1095237632 | bytes 18644992 | tf_op jit(solution)/shard_map/hgqk,khd->qhgd/dot_general | solution.py:39
  45.8 6.0 %fusion.60 = bf16[8,512,128]{1,2,0:T(8,128)(2,1)S(1)} fusion(f32[8,512]{1,0:T(8,128)S(1)} %fusion.18, f32[8,512]{1,0:T(8,128)S(1)} %get-tuple-element.87, f32[512,512,8]{1,0,2:T(8,128)} %copy-done.4, pred[512,512]{0,1:T(8,128)(4,1)S(1)} %iota_compare_fusion.1, bf16[1,1024,128]{2,1,0:T(8,128)(2,1)S(1)} %copy-done.10), kind=kOutput, calls=%fused_computation.73 | convolution fusion | flops 547880960 | bytes 9863168 | tf_op jit(solution)/shard_map/hgqk,khd->qhgd/dot_general | solution.py:39
  51.8 14.7 %convert_bitcast_fusion = bf16[4096,1024]{0,1:T(8,128)(2,1)} fusion(bf16[1024,4096]{1,0:T(8,128)(2,1)} %param.23, bf16[512,1024]{0,1:T(8,128)(2,1)S(1)} %bitcast.327, bf16[512,1024]{0,1:T(8,128)(2,1)S(1)} %bitcast.328), kind=kOutput, calls=%fused_computation.23 | convolution fusion | flops 8598323200 | bytes 18874368 | tf_op jit(solution)/shard_map/dot_general | solution.py:109
  67.0 93.9 %all-gather.12.cloned.1.call-done = bf16[1,1024,4096]{2,1,0:T(8,128)(2,1)} async-done(((bf16[1,128,4096]{2,1,0:T(8,128)(2,1)}), bf16[1,1024,4096]{2,1,0:T(8,128)(2,1)}) %all-gather.12.cloned.1.call-update) | async-done | bytes 8388624 | tf_op jit(solution)/shard_map/all_gather | solution.py:117
  160.9 9.1 %fusion.63 = bf16[1024,512]{0,1:T(8,128)(2,1)S(1)} fusion(bf16[4096,512]{1,0:T(8,128)(2,1)} %all-gather.8.cloned.1.call-done, bf16[1,1024,4096]{2,1,0:T(8,128)(2,1)} %all-gather.12.cloned.1.call-done), kind=kOutput, calls=%fused_computation.74 | convolution fusion | flops 4295491584 | bytes 13631488 | tf_op jit(solution)/shard_map/dot_general | solution.py:124
  170.0 23.1 %all-gather.6.cloned.1.call-done = bf16[4096,128]{1,0:T(8,128)(2,1)} async-done(((bf16[256,128]{1,0:T(8,128)(2,1)}), bf16[4096,128]{1,0:T(8,128)(2,1)}) %all-gather.6.cloned.1.call-update) | async-done | bytes 1048592 | tf_op jit(solution)/shard_map/all_gather | solution.py:120
  193.1 5.9 %fusion.77 = bf16[1024,128]{1,0:T(8,128)(2,1)S(1)} fusion(bf16[4096,128]{1,0:T(8,128)(2,1)} %all-gather.6.cloned.1.call-done, bf16[1,1024,4096]{2,1,0:T(8,128)(2,1)} %all-gather.12.cloned.1.call-done), kind=kOutput, calls=%fused_computation.83 | convolution fusion | flops 1073872896 | bytes 9699328 | tf_op jit(solution)/shard_map/dot_general | solution.py:127
  199.9 2.0 copy-done.1
  202.8 24.4 %all-gather.10.cloned.1.call-done = bf16[4096,128]{1,0:T(8,128)(2,1)} async-done(((bf16[256,128]{1,0:T(8,128)(2,1)}), bf16[4096,128]{1,0:T(8,128)(2,1)}) %all-gather.10.cloned.1.call-update) | async-done | bytes 1048592 | tf_op jit(solution)/shard_map/all_gather | solution.py:121
  227.2 6.1 %fusion.80 = bf16[1024,128]{1,0:T(8,128)(2,1)S(1)} fusion(bf16[4096,128]{1,0:T(8,128)(2,1)} %all-gather.10.cloned.1.call-done, bf16[1,1024,4096]{2,1,0:T(8,128)(2,1)} %all-gather.12.cloned.1.call-done), kind=kOutput, calls=%fused_computation.84 | convolution fusion | flops 1073872896 | bytes 9699328 | tf_op jit(solution)/shard_map/dot_general | solution.py:130
  233.3 2.5 fusion.51
  235.9 1.6 copy.44
  237.4 1.8 fusion.22
  239.2 1.9 fusion.17
  241.1 1.6 copy-done
  242.7 3.5 fusion.36
  246.3 2.5 copy.45
  248.8 97.0 %reduce-scatter.3.cloned.1.call-done = bf16[512,1024]{0,1:T(8,128)(2,1)} async-done(((bf16[4096,1024]{0,1:T(8,128)(2,1)}), bf16[512,1024]{0,1:T(8,128)(2,1)}) %reduce-scatter.3.cloned.1.call-update) | async-done | bytes 1048592 | tf_op jit(solution)/shard_map/reduce_scatter | solution.py:108
  345.8 1.9 fusion.45
  348.8 4.1 fusion.28
  352.9 1.5 fusion.43
  358.1 5.3 %fusion.2 = (f32[4,512]{1,0:T(4,128)S(1)}, f32[1024,512,4]{1,0,2:T(8,128)S(1)}) fusion(f32[4,512]{1,0:T(4,128)S(1)} %fusion.17, f32[4,512]{1,0:T(4,128)S(1)} %get-tuple-element.81, f32[1024,512,4]{1,0,2:T(8,128)} %copy-done, pred[512,1024]{0,1:T(8,128)(4,1)S(1)} %iota_compare_fusion, bf16[512,4,128]{0,2,1:T(8,128)(2,1)S(1)} %bitcast.320, ...), kind=kOutput, calls=%fused_computation.9 | convolution fusion | flops 549451776 | bytes 18112512 | tf_op jit(solution)/shard_map/qhgd,khd->hgqk/dot_general | solution.py:66
  364.2 3.1 fusion.27
  369.6 2.9 fusion.87
  372.6 8.6 %fusion.24 = bf16[4096,768]{0,1:T(8,128)(2,1)} fusion(bf16[1,1024,4096]{2,1,0:T(8,128)(2,1)S(1)} %bitcast.326, bf16[1024,128]{0,1:T(8,128)(2,1)S(1)} %fusion.87, bf16[1024,128]{0,1:T(8,128)(2,1)S(1)} %fusion.90, bf16[512,512]{0,1:T(8,128)(2,1)S(1)} %bitcast.319, bf16[512,512]{0,1:T(8,128)(2,1)S(1)} %bitcast.324), kind=kOutput, calls=%fused_computation.33 | convolution fusion | flops 6451888128 | bytes 16252928 | tf_op jit(solution)/shard_map/dot_general | solution.py:139
  381.2 69.0 %reduce-scatter.5.cloned.1.call-done = bf16[256,768]{0,1:T(8,128)(2,1)} async-done(((bf16[4096,768]{0,1:T(8,128)(2,1)}), bf16[256,768]{0,1:T(8,128)(2,1)}) %reduce-scatter.5.cloned.1.call-update) | async-done | bytes 393232 | tf_op jit(solution)/shard_map/reduce_scatter | solution.py:142
  (63 shorter events, 19.7 us)
Async XLA Ops:
  7.2 59.8 %all-gather.8.cloned.1.call-start = ((), (), s32[]{:S(2)}) async-start(), calls=%async_computation.3 | async-start | bytes 4456448 | tf_op jit(solution)/shard_map/all_gather | solution.py:119
  7.9 153.0 %all-gather.12.cloned.1.call-start = ((), (), s32[]{:S(2)}) async-start(), calls=%async_computation.7 | async-start | bytes 9437184 | tf_op jit(solution)/shard_map/all_gather | solution.py:117
  8.6 184.5 %all-gather.6.cloned.1.call-start = ((), (), s32[]{:S(2)}) async-start(), calls=%async_computation.2 | async-start | bytes 1114112 | tf_op jit(solution)/shard_map/all_gather | solution.py:120
  9.4 217.9 %all-gather.10.cloned.1.call-start = ((), (), s32[]{:S(2)}) async-start(), calls=%async_computation.4 | async-start | bytes 1114112 | tf_op jit(solution)/shard_map/all_gather | solution.py:121
  10.0 335.8 %reduce-scatter.3.cloned.1.call-start = ((), (), s32[]{:S(2)}) async-start(), calls=%async_computation.5 | async-start | bytes 9437184 | tf_op jit(solution)/shard_map/reduce_scatter | solution.py:108
  10.1 5.3 %copy-start.5 = (bf16[1,1024,128]{2,1,0:T(8,128)(2,1)S(1)}, bf16[1,1024,128]{2,1,0:T(8,128)(2,1)}, u32[]{:S(2)}) copy-start(bf16[1,1024,128]{2,1,0:T(8,128)(2,1)} %param.21) | copy-start | bytes 786436
  16.9 3.2 copy-start.4
  27.6 9.4 %copy-start.10 = (bf16[1,1024,128]{2,1,0:T(8,128)(2,1)S(1)}, bf16[1,1024,128]{2,1,0:T(8,128)(2,1)}, u32[]{:S(2)}) copy-start(bf16[1,1024,128]{2,1,0:T(8,128)(2,1)} %param.22) | copy-start | bytes 786436
  66.5 383.7 %reduce-scatter.5.cloned.1.call-start = ((), (), s32[]{:S(2)}) async-start(), calls=%async_computation.6 | async-start | bytes 6684672 | tf_op jit(solution)/shard_map/reduce_scatter | solution.py:142
  199.9 2.0 copy-start.1
  227.2 6.1 %copy-start.2 = (f32[512,512,4]{1,0,2:T(8,128)S(1)}, f32[512,512,4]{1,0,2:T(8,128)}, u32[]{:S(2)}) copy-start(f32[512,512,4]{1,0,2:T(8,128)} %copy-done.1) | copy-start | bytes 12582916
  239.2 3.5 copy-start
  348.8 4.1 copy-start.3
  354.4 2.1 copy-start.8
  358.1 5.4 %copy-start.6 = (bf16[512,512]{0,1:T(8,128)(2,1)}, bf16[512,512]{0,1:T(8,128)(2,1)S(1)}, u32[]{:S(2)}) copy-start(bf16[512,512]{0,1:T(8,128)(2,1)S(1)} %copy.97) | copy-start | bytes 1572868
  358.1 5.4 %slice-start = ((s8[8388608]{0:T(1024)(128)(4,1)}), s8[4194304]{0:T(1024)(128)(4,1)S(1)}, s32[]{:S(2)}) async-start(s8[8388608]{0:T(1024)(128)(4,1)} %bitcast.309), calls=%async_computation.8 | async-start | bytes 8388608
  358.1 6.1 %slice-start.1 = ((s8[8388608]{0:T(1024)(128)(4,1)}), s8[4194304]{0:T(1024)(128)(4,1)S(1)}, s32[]{:S(2)}) async-start(s8[8388608]{0:T(1024)(128)(4,1)} %bitcast.309), calls=%async_computation.9 | async-start | bytes 8388608
  367.4 2.3 copy-start.7
  368.1 4.4 slice-start.2
  369.6 2.9 copy-start.9
  369.6 2.9 slice-start.3
Sparse Core Ops, SparseCore 0:
  9.7 39.8 all-gather.7
  52.0 108.8 all-gather.11
  162.6 30.5 all-gather.5
  194.7 32.5 all-gather.9
  231.0 114.7 reduce-scatter.2
  381.4 68.7 reduce-scatter.4
where the time goes:
time: 471 us; the launch traced here: 462 us
  waiting for transfers between devices  310 us (66%)
  matrix products  94.9 us (20%)
  other arithmetic  20.9 us (4%)
  local copies, waits for them, and re-layouts  20.5 us (4%)
  between operations  14.7 us (3%)
    reduce_scatter x1, waiting for transfers between devices, per_device(): lax.psum_scatter(lax.dot_general(projector, context_t, (((0,), (1,)), (()...  97 us
    all_gather x1, waiting for transfers between devices, per_device(): rows_all = lax.all_gather(student_inputs[0], 'tensor', axis=0, tiled=True)  93.9 us
    reduce_scatter x1, waiting for transfers between devices, per_device(): lax.psum_scatter(whole.astype(jnp.bfloat16), 'dp', scatter_dimension=0, t...  69 us
    all_gather x1, waiting for transfers between devices, per_device(): lax.all_gather(value_weight, 'dp', axis=0, tiled=True)  24.4 us
    all_gather x1, waiting for transfers between devices, per_device(): lax.all_gather(key_weight, 'dp', axis=0, tiled=True)  23.1 us
    dot_general x4, matrix products, attend(): jnp.einsum('hgqk,khd->qhgd', rounded, value_heads[:limit], preferred_elem...  20.9 us
    dot_general x1, matrix products, per_device(): lax.dot_general(projector, context_t, (((0,), (1,)), ((), ())), preferred...  14.7 us
    reduce_sum x4, other arithmetic, attend(): probs = shifted / jnp.sum(shifted, axis=-1, keepdims=True)  14 us
  transfers between devices with their start and end apart: 6, of which 5 were waited for; matrix products, arithmetic and copies ran while one was open for 20% of the time, Pallas kernels for 0%

commit v1 on v0

v1 whole, which is shorter than its diff:
```python
import jax
import jax.numpy as jnp
from jax import lax
from jax.experimental import pallas as pl
from jax.experimental.pallas import tpu as pltpu
from jax.sharding import Mesh, PartitionSpec as P

HEAD = 128
FACTOR = HEAD ** (-0.5)
LOG2E = 1.4426950408889634
BLOCK = 256
SEQ = 1024
DP = ("ylo", "z", "core")
TENSOR = ("x", "yhi")
NT = (((1,), (1,)), ((), ()))
VMEM = pltpu.CompilerParams(vmem_limit_bytes=48 * 1024 * 1024)


def dot(a, b):
    return jnp.dot(a, b, preferred_element_type=jnp.float32)


def teacher_kernel(q_ref, k_ref, v_ref, o_ref):
    for number in range(SEQ // BLOCK):
        first = number * BLOCK
        limit = first + BLOCK
        scores = lax.dot_general(
            q_ref[first:limit, :], k_ref[:limit, :], NT, preferred_element_type=jnp.float32
        )
        row = first + lax.broadcasted_iota(jnp.int32, scores.shape, 0)
        col = lax.broadcasted_iota(jnp.int32, scores.shape, 1)
        scores = jnp.where(col <= row, scores, -1e30)
        top = jnp.max(scores, axis=1, keepdims=True)
        weights = jnp.exp2((scores - top) * (FACTOR * LOG2E))
        total = jnp.sum(weights, axis=1, keepdims=True)
        context = dot(weights.astype(jnp.bfloat16), v_ref[:limit, :])
        o_ref[first:limit, :] = (context / total).astype(jnp.bfloat16)


def teacher_attention(queries, keys, values, first, count):
    return pl.pallas_call(
        teacher_kernel,
        grid=(count,),
        in_specs=[
            pl.BlockSpec((SEQ, HEAD), lambda h: (0, first + h)),
            pl.BlockSpec((SEQ, HEAD), lambda h: (0, 0)),
            pl.BlockSpec((SEQ, HEAD), lambda h: (0, 0)),
        ],
        out_specs=pl.BlockSpec((SEQ, HEAD), lambda h: (0, h)),
        out_shape=jax.ShapeDtypeStruct((SEQ, count * HEAD), jnp.bfloat16),
        compiler_params=VMEM,
        name="teacher_attention",
    )(queries, keys, values)


def project_kernel(a_ref, b_ref, p_ref, o_ref):
    half = a_ref.shape[1]
    o_ref[0] = (dot(a_ref[...], p_ref[:half, :]) + dot(b_ref[...], p_ref[half:, :])).astype(
        jnp.bfloat16
    )


def project(context_a, context_b, projector, part):
    rows = projector.shape[0]
    return pl.pallas_call(
        project_kernel,
        grid=(8,),
        in_specs=[
            pl.BlockSpec(context_a.shape, lambda g: (0, 0)),
            pl.BlockSpec(context_b.shape, lambda g: (0, 0)),
            pl.BlockSpec((rows, 256), lambda g: (0, 2 * g + part)),
        ],
        out_specs=pl.BlockSpec((1, SEQ, 256), lambda g: (g, 0, 0)),
        out_shape=jax.ShapeDtypeStruct((8, SEQ, 256), jnp.bfloat16),
        compiler_params=VMEM,
        name="project",
    )(context_a, context_b, projector)


def student_kernel(has_start, y_ref, q_ref, k_ref, v_ref, mine_ref, theirs_ref, *rest):
    if has_start:
        start_ref, gq_ref, gkv_ref, kt, vt, dk, dv = rest
    else:
        gq_ref, gkv_ref, kt, vt, dk, dv = rest
    step = pl.program_id(0)

    @pl.when(step == 0)
    def _():
        kt[...] = k_ref[...].T
        vt[...] = v_ref[...].T
        if has_start:
            dk[...] = start_ref[:, :HEAD]
            dv[...] = start_ref[:, HEAD:]
        else:
            dk[...] = jnp.zeros_like(dk)
            dv[...] = jnp.zeros_like(dv)

    for number in range(SEQ // BLOCK):
        first = number * BLOCK
        limit = first + BLOCK
        queries = q_ref[first:limit, :]
        scores = lax.dot_general(k_ref[:limit, :], queries, NT, preferred_element_type=jnp.float32)
        key = lax.broadcasted_iota(jnp.int32, scores.shape, 0)
        query = first + lax.broadcasted_iota(jnp.int32, scores.shape, 1)
        scores = jnp.where(key <= query, scores, -1e30)
        top = jnp.max(scores, axis=0, keepdims=True)
        weights = jnp.exp2((scores - top) * (FACTOR * LOG2E))
        probs = weights * (1.0 / jnp.sum(weights, axis=0, keepdims=True))
        rounded = probs.astype(jnp.bfloat16)
        context = dot(vt[:, :limit], rounded).T
        target = mine_ref[0, first:limit, :].astype(jnp.float32) + theirs_ref[
            first:limit, :
        ].astype(jnp.float32)
        incoming = ((context - target) * (1.0 / 16)).astype(jnp.bfloat16)
        grad_probs = lax.dot_general(
            v_ref[:limit, :], incoming, NT, preferred_element_type=jnp.float32
        )
        inner = jnp.sum(grad_probs * probs, axis=0, keepdims=True)
        scaled = (probs * (grad_probs - inner) * FACTOR).astype(jnp.bfloat16)
        dv[:limit, :] += dot(rounded, incoming)
        dk[:limit, :] += dot(scaled, queries)
        gq_ref[first:limit, :] = dot(kt[:, :limit], scaled).T.astype(jnp.bfloat16)

    @pl.when(step == pl.num_programs(0) - 1)
    def _():
        gkv_ref[:, :HEAD] = dk[...].astype(gkv_ref.dtype)
        gkv_ref[:, HEAD:] = dv[...].astype(gkv_ref.dtype)


def student_attention(y, projected, mine, theirs, part, start=None):
    specs = [
        pl.BlockSpec((SEQ, HEAD), lambda h, y: (0, 2 * part + h)),
        pl.BlockSpec((SEQ, HEAD), lambda h, y: (0, 4)),
        pl.BlockSpec((SEQ, HEAD), lambda h, y: (0, 5)),
        pl.BlockSpec((1, SEQ, HEAD), lambda h, y: (y[0], 0, h)),
        pl.BlockSpec((SEQ, HEAD), lambda h, y: (0, h)),
    ]
    operands = [projected, projected, projected, mine, theirs]
    if start is not None:
        specs.append(pl.BlockSpec((SEQ, 2 * HEAD), lambda h, y: (0, 0)))
        operands.append(start)
    return pl.pallas_call(
        lambda *refs: student_kernel(start is not None, *refs),
        grid_spec=pltpu.PrefetchScalarGridSpec(
            num_scalar_prefetch=1,
            grid=(2,),
            in_specs=specs,
            out_specs=[
                pl.BlockSpec((SEQ, HEAD), lambda h, y: (0, h)),
                pl.BlockSpec((SEQ, 2 * HEAD), lambda h, y: (0, 0)),
            ],
            scratch_shapes=[
                pltpu.VMEM((HEAD, SEQ), jnp.bfloat16),
                pltpu.VMEM((HEAD, SEQ), jnp.bfloat16),
                pltpu.VMEM((SEQ, HEAD), jnp.float32),
                pltpu.VMEM((SEQ, HEAD), jnp.float32),
            ],
        ),
        out_shape=[
            jax.ShapeDtypeStruct((SEQ, 2 * HEAD), jnp.bfloat16),
            jax.ShapeDtypeStruct(
                (SEQ, 2 * HEAD), jnp.float32 if start is None else jnp.bfloat16
            ),
        ],
        compiler_params=VMEM,
        name="student_attention",
    )(y, *operands)


def shift(array, axis, step=1):
    n = lax.axis_size(axis)
    return lax.ppermute(array, axis, [(i, (i + step) % n) for i in range(n)])


def swap_core(whole):
    parts = whole.astype(jnp.bfloat16).reshape(8, 2, 256, whole.shape[1])
    c = lax.axis_index("core")
    theirs = lax.dynamic_index_in_dim(parts, 1 - c, 1, keepdims=False)
    mine = lax.dynamic_index_in_dim(parts, c, 1, keepdims=False)
    return mine.astype(jnp.float32) + shift(theirs, "core").astype(jnp.float32)


def reduce_ring(whole):
    cols = whole.shape[1]
    pair = swap_core(whole).astype(jnp.bfloat16)
    pair = pair.reshape(2, 4, 256, cols).transpose(1, 0, 2, 3).reshape(4, 512, cols)
    summed = lax.psum_scatter(pair, "z", scatter_dimension=0, tiled=True).reshape(2, 256, cols)
    y = lax.axis_index("ylo")
    theirs = lax.dynamic_index_in_dim(summed, 1 - y, 0, keepdims=False)
    mine = lax.dynamic_index_in_dim(summed, y, 0, keepdims=False)
    return mine.astype(jnp.float32) + shift(theirs, "ylo").astype(jnp.float32)


def reduce_direct(whole):
    pair = swap_core(whole).astype(jnp.bfloat16)
    y = lax.axis_index("ylo")
    z = lax.axis_index("z")
    total = lax.dynamic_index_in_dim(pair, y * 4 + z, 0, keepdims=False).astype(jnp.float32)
    for dy in range(2):
        for dz in range(4):
            if dy or dz:
                there = (y + dy) % 2 * 4 + (z + dz) % 4
                route = [
                    (i * 4 + k, (i + dy) % 2 * 4 + (k + dz) % 4) for i in range(2) for k in range(4)
                ]
                sent = lax.dynamic_index_in_dim(pair, there, 0, keepdims=False)
                total += lax.ppermute(sent, ("ylo", "z"), route).astype(jnp.float32)
    return total


def per_device(
    teacher_queries,
    teacher_keys,
    teacher_values,
    projector,
    student_inputs,
    query_weight,
    key_weight,
    value_weight,
):
    tq, tk, tv = teacher_queries[0], teacher_keys[0], teacher_values[0]
    yhi = lax.axis_index("yhi")
    own = student_inputs[0]
    weights = lax.all_gather(
        jnp.concatenate([query_weight, key_weight, value_weight], axis=1), DP, axis=0, tiled=True
    )
    other = shift(own, "yhi")
    own_all = lax.all_gather(own, "x", axis=0, tiled=True)
    other_all = lax.all_gather(other, "x", axis=0, tiled=True)

    context_a = teacher_attention(tq, tk, tv, 0, 4)
    tq, other = lax.optimization_barrier((tq, other))
    context_b = teacher_attention(tq, tk, tv, 4, 4)
    context_b, own_all, weights = lax.optimization_barrier((context_b, own_all, weights))
    sums = []
    for part in range(2):
        product = project(context_a, context_b, projector, part)
        sums.append(
            lax.psum_scatter(product, "x", scatter_dimension=0, tiled=True)
        )

    pieces = jnp.stack([own_all.reshape(4, 128, -1), other_all.reshape(4, 128, -1)], axis=1)
    flipped = jnp.stack([other_all.reshape(4, 128, -1), own_all.reshape(4, 128, -1)], axis=1)
    rows_all = jnp.where(yhi == 0, pieces, flipped).reshape(SEQ, -1)
    projected = dot(rows_all, weights).astype(jnp.bfloat16)

    y = yhi.astype(jnp.int32).reshape(1)
    theirs = [
        shift(lax.dynamic_index_in_dim(s, 1 - yhi, 0, keepdims=False), "yhi") for s in sums
    ]
    across = (((0,), (0,)), ((), ()))
    grad_a, part_kv = student_attention(y, projected, sums[0], theirs[0], 0)
    out_a = reduce_ring(
        lax.dot_general(rows_all, grad_a, across, preferred_element_type=jnp.float32)
    )
    grad_b, grad_kv = student_attention(y, projected, sums[1], theirs[1], 1, part_kv)
    out_b = reduce_direct(
        lax.dot_general(
            rows_all,
            jnp.concatenate([grad_b, grad_kv], axis=1),
            across,
            preferred_element_type=jnp.float32,
        )
    )
    return jnp.concatenate([out_a, out_b[:, :256]], axis=1), out_b[:, 256:384], out_b[:, 384:]


def solution(mesh):
    fine = Mesh(mesh.devices.reshape(2, 4, 2, 4, 2), DP + TENSOR)
    placed = (
        P(DP, None, TENSOR),
        P(DP, None, TENSOR),
        P(DP, None, TENSOR),
        P(TENSOR, None),
        P(DP, TENSOR, None),
        P(DP, TENSOR),
        P(DP, TENSOR),
        P(DP, TENSOR),
    )
    return jax.shard_map(
        per_device,
        mesh=fine,
        in_specs=placed,
        out_specs=(P(DP, TENSOR), P(DP, TENSOR), P(DP, TENSOR)),
        check_vma=False,
    )
```

time: 471 us -> 361 us (0.77); the launches traced: 462 us -> 360 us
  waiting for transfers between devices: 310 us -> 210 us
  matrix products: 94.9 us -> 21.8 us
  Pallas kernels: 0 us -> 55 us
  starting transfers between devices: 0.64 us -> 24.5 us
  local copies, waits for them, and re-layouts: 20.5 us -> 14.4 us
    reduce_scatter x2 -> x3, waiting for transfers between devices: 166 us -> 71.8 us  [the longest x2 71.8 us: per_device(): sums.append(lax.psum_scatter(product, 'x', scatter_dimension=0, tiled=True))]
    dot_general x21 -> x3, matrix products: 94.9 us -> 21.8 us  [the longest x1 11 us: dot(): return jnp.dot(a, b, preferred_element_type=jnp.float32)]
    all_gather x4 -> x3, waiting for transfers between devices: 141 us -> 83.4 us  [the longest x1 45.1 us: per_device(): lax.all_gather(jnp.concatenate([query_weight, key_weight, value_weight],...]
    pallas_call x0 -> x6, Pallas kernels: none -> 55 us  [the longest x2 22 us: student_attention(): pl.pallas_call(lambda *refs: student_kernel(start is not None, *refs), gr...]
    ppermute x0 -> x13, waiting for transfers between devices: none -> 53.6 us  [the longest x6 28.9 us: shift(): return lax.ppermute(array, axis, [(i, (i + step) % n) for i in range(n)])]
    ppermute x0 -> x13, starting transfers between devices: none -> 24.2 us  [the longest x7 13.2 us: reduce_direct(): total += lax.ppermute(sent, ('ylo', 'z'), route).astype(jnp.float32)]
    reduce_sum x4 -> x0, other arithmetic: 14 us -> none  [attend(): probs = shifted / jnp.sum(shifted, axis=-1, keepdims=True)]
    select_n x0 -> x1, other arithmetic: none -> 10.7 us  [per_device(): rows_all = jnp.where(yhi == 0, pieces, flipped).reshape(SEQ, -1)]
  transfers between devices with their start and end apart: 6 -> 19, of which waited for: 5 -> 14; matrix products, arithmetic and copies ran while one was open for 20% -> 13% of each run, Pallas kernels for 0% -> 15%
where the time goes in v1:
time: 361 us; the launch traced here: 360 us
  waiting for transfers between devices  210 us (58%)
  Pallas kernels  55 us (15%)
  starting transfers between devices  24.5 us (7%)
  matrix products  21.8 us (6%)
  other arithmetic  20.2 us (6%)
  between operations  14.5 us (4%)
  local copies, waits for them, and re-layouts  14.4 us (4%)
    reduce_scatter x2, waiting for transfers between devices, per_device(): sums.append(lax.psum_scatter(product, 'x', scatter_dimension=0, tiled=True))  71.8 us
    all_gather x1, waiting for transfers between devices, per_device(): lax.all_gather(jnp.concatenate([query_weight, key_weight, value_weight],...  45.1 us
    all_gather x1, waiting for transfers between devices, per_device(): other_all = lax.all_gather(other, 'x', axis=0, tiled=True)  31.9 us
    ppermute x6, waiting for transfers between devices, shift(): return lax.ppermute(array, axis, [(i, (i + step) % n) for i in range(n)])  28.9 us
    ppermute x7, waiting for transfers between devices, reduce_direct(): total += lax.ppermute(sent, ('ylo', 'z'), route).astype(jnp.float32)  24.7 us
    pallas_call x2, Pallas kernels, student_attention(): pl.pallas_call(lambda *refs: student_kernel(start is not None, *refs), gr...  22 us
    pallas_call x2, Pallas kernels, project(): pl.pallas_call(project_kernel, grid=(8,), in_specs=[pl.BlockSpec(context_...  18.7 us
    pallas_call x2, Pallas kernels, teacher_attention(): pl.pallas_call(teacher_kernel, grid=(count,), in_specs=[pl.BlockSpec((SEQ...  14.3 us
  transfers between devices with their start and end apart: 19, of which 14 were waited for; matrix products, arithmetic and copies ran while one was open for 13% of the time, Pallas kernels for 15%

profile of v1, /device:TPU:0, one launch (start us, length us, event | category | flops | bytes accessed | tf_op | source)
XLA Modules:
  0.0 359.9 jit_solution(16059853918649783168)
XLA Ops:
  9.8 3.4 collective-permute-start
  13.2 23.4 %collective-permute-done = bf16[128,4096]{1,0:T(8,128)(2,1)S(1)} collective-permute-done((bf16[128,4096]{1,0:T(8,128)(2,1)}, bf16[128,4096]{1,0:T(8,128)(2,1)S(1)}, u32[]{:S(2)}, u32[]{:S(2)}) %collective-permute-start) | collective-permute-done | bytes 1048608 | tf_op jit(solution)/shard_map/ppermute | solution.py:172
  39.7 7.1 %teacher_attention.3.a_ref = bf16[1024,512]{1,0:T(8,128)(2,1)S(1)} custom-call(bf16[1024,1024]{1,0:T(8,128)(2,1)S(1)} %bitcast.59, bf16[1024,128]{1,0:T(8,128)(2,1)S(1)} %bitcast.61, bf16[1024,128]{1,0:T(8,128)(2,1)S(1)} %bitcast.63), custom_call_target="tpu_custom_call" | custom-call | tf_op jit(solution)/shard_map/teacher_attention/pallas_call | solution.py:41
  46.8 7.2 %teacher_attention.2.b_ref = bf16[1024,512]{1,0:T(8,128)(2,1)S(1)} custom-call(bf16[1024,1024]{1,0:T(8,128)(2,1)S(1)} %bitcast.60, bf16[1024,128]{1,0:T(8,128)(2,1)S(1)} %bitcast.62, bf16[1024,128]{1,0:T(8,128)(2,1)S(1)} %bitcast.64), custom_call_target="tpu_custom_call" | custom-call | tf_op jit(solution)/shard_map/teacher_attention/pallas_call | solution.py:41
  54.0 6.4 %all-gather.9.cloned.1.call-done = bf16[1,512,4096]{2,1,0:T(8,128)(2,1)} async-done(((bf16[1,128,4096]{2,1,0:T(8,128)(2,1)}), bf16[1,512,4096]{2,1,0:T(8,128)(2,1)}) %all-gather.9.cloned.1.call-update) | async-done | bytes 4194320 | tf_op jit(solution)/shard_map/all_gather | solution.py:228
  60.4 45.1 %all-gather.5.cloned.1.call-done = bf16[4096,768]{1,0:T(8,128)(2,1)} async-done(((bf16[256,768]{1,0:T(8,128)(2,1)}), bf16[4096,768]{1,0:T(8,128)(2,1)}) %all-gather.5.cloned.1.call-update) | async-done | bytes 6291472 | tf_op jit(solution)/shard_map/all_gather | solution.py:224
  105.5 9.3 %project.2 = bf16[8,1024,256]{2,1,0:T(8,128)(2,1)} custom-call(bf16[1024,512]{1,0:T(8,128)(2,1)S(1)} %teacher_attention.3.a_ref, bf16[1024,512]{1,0:T(8,128)(2,1)S(1)} %teacher_attention.2.b_ref, bf16[1024,4096]{1,0:T(8,128)(2,1)} %p_ref.3), custom_call_target="tpu_custom_call" | custom-call | tf_op jit(solution)/shard_map/project/pallas_call | solution.py:65
  114.8 9.4 %project.3 = bf16[8,1024,256]{2,1,0:T(8,128)(2,1)} custom-call(bf16[1024,512]{1,0:T(8,128)(2,1)S(1)} %teacher_attention.3.a_ref, bf16[1024,512]{1,0:T(8,128)(2,1)S(1)} %teacher_attention.2.b_ref, bf16[1024,4096]{1,0:T(8,128)(2,1)} %p_ref.3), custom_call_target="tpu_custom_call" | custom-call | tf_op jit(solution)/shard_map/project/pallas_call | solution.py:65
  124.4 31.9 %all-gather.7.cloned.1.call-done = bf16[512,4096]{1,0:T(8,128)(2,1)} async-done(((bf16[128,4096]{1,0:T(8,128)(2,1)}), bf16[512,4096]{1,0:T(8,128)(2,1)}) %all-gather.7.cloned.1.call-update) | async-done | bytes 4194320 | tf_op jit(solution)/shard_map/all_gather | solution.py:229
  156.3 10.7 %maximum_select_fusion = bf16[4,2,128,4096]{3,2,1,0:T(8,128)(2,1)} fusion(bf16[4,1,128,4096]{3,2,1,0:T(8,128)(2,1)} %bitcast.71, bf16[4,1,128,4096]{3,2,1,0:T(8,128)(2,1)} %bitcast.70, pred[]{:T(512)S(6)} %eq.18), kind=kLoop, calls=%fused_computation | loop fusion | flops 12582912 | bytes 16777216 | tf_op jit(solution)/shard_map/jit(_where)/select_n | solution.py:244
  167.0 38.7 %reduce-scatter.4.cloned.1.call-done.refs_4_ = bf16[2,1024,256]{2,1,0:T(8,128)(2,1)} async-done(((bf16[8,1024,256]{2,1,0:T(8,128)(2,1)}), bf16[2,1024,256]{2,1,0:T(8,128)(2,1)}) %reduce-scatter.4.cloned.1.call-update) | async-done | bytes 1048592 | tf_op jit(solution)/shard_map/reduce_scatter | solution.py:239
  205.7 1.9 dynamic-slice_bitcast_fusion.3
  207.5 3.0 collective-permute-start.1
  210.6 11.0 %convolution_convert_fusion.2.refs_1_.refs_2_.refs_3_ = bf16[1024,768]{1,0:T(8,128)(2,1)S(1)} fusion(bf16[1024,4096]{1,0:T(8,128)(2,1)} %bitcast.65, bf16[4096,768]{1,0:T(8,128)(2,1)} %all-gather.5.cloned.1.call-done), kind=kOutput, calls=%fused_computation.8 | convolution fusion | flops 6443237376 | bytes 16252928 | tf_op jit(solution)/shard_map/dot_general | solution.py:20
  221.5 33.1 %reduce-scatter.8.cloned.1.call-done.refs_4_ = bf16[2,1024,256]{2,1,0:T(8,128)(2,1)} async-done(((bf16[8,1024,256]{2,1,0:T(8,128)(2,1)}), bf16[2,1024,256]{2,1,0:T(8,128)(2,1)}) %reduce-scatter.8.cloned.1.call-update) | async-done | bytes 1048592 | tf_op jit(solution)/shard_map/reduce_scatter | solution.py:239
  255.7 3.3 collective-permute-start.4
  259.0 11.0 %student_attention.2 = (bf16[1024,256]{1,0:T(8,128)(2,1)S(1)}, f32[1024,256]{1,0:T(8,128)S(1)}) custom-call(s32[1]{0:T(128)} %bitcast.8.refs_0_, bf16[1024,768]{1,0:T(8,128)(2,1)S(1)} %convolution_convert_fusion.2.refs_1_.refs_2_.refs_3_, bf16[1024,768]{1,0:T(8,128)(2,1)S(1)} %convolution_convert_fusion.2.refs_1_.refs_2_.refs_3_, ...), custom_call_target="tpu_custom_call" | custom-call | tf_op jit(solution)/shard_map/student_attention/pallas_call | solution.py:142
  270.0 6.0 %convolution_convert_fusion.1 = bf16[4096,256]{1,0:T(8,128)(2,1)S(1)} fusion(bf16[1024,4096]{1,0:T(8,128)(2,1)} %bitcast.66, bf16[1024,256]{1,0:T(8,128)(2,1)S(1)} %get-tuple-element.15), kind=kOutput, calls=%fused_computation.2 | convolution fusion | flops 2148532224 | bytes 11010048 | tf_op jit(solution)/shard_map/dot_general | solution.py:254
  277.4 11.0 %student_attention.3 = (bf16[1024,256]{1,0:T(8,128)(2,1)S(1)}, bf16[1024,256]{1,0:T(8,128)(2,1)S(1)}) custom-call(s32[1]{0:T(128)} %bitcast.8.refs_0_, bf16[1024,768]{1,0:T(8,128)(2,1)S(1)} %convolution_convert_fusion.2.refs_1_.refs_2_.refs_3_, bf16[1024,768]{1,0:T(8,128)(2,1)S(1)} %convolution_convert_fusion.2.refs_1_.refs_2_.refs_3_, ...), custom_call_target="tpu_custom_call" | custom-call | tf_op jit(solution)/shard_map/student_attention/pallas_call | solution.py:142
  288.5 4.8 %convolution_convert_fusion = bf16[4096,512]{1,0:T(8,128)(2,1)S(1)} fusion(bf16[1024,4096]{1,0:T(8,128)(2,1)S(1)} %bitcast.69, bf16[1024,256]{1,0:T(8,128)(2,1)S(1)} %get-tuple-element.18, bf16[1024,256]{1,0:T(8,128)(2,1)S(1)} %get-tuple-element.17), kind=kOutput, calls=%fused_computation.1 | convolution fusion | flops 4299161600 | bytes 13631488 | tf_op jit(solution)/shard_map/dot_general | solution.py:258
  293.3 2.1 copy-done.6
  299.6 1.8 collective-permute-done.5
  301.5 2.9 fusion
  305.3 3.0 collective-permute-start.12
  312.2 2.3 collective-permute-start.8
  315.4 3.1 collective-permute-start.7
  318.6 4.1 %collective-permute-done.11 = bf16[256,512]{1,0:T(8,128)(2,1)S(1)} collective-permute-done((bf16[256,512]{1,0:T(8,128)(2,1)S(1)}, bf16[256,512]{1,0:T(8,128)(2,1)S(1)}, u32[]{:S(2)}, u32[]{:S(2)}) %collective-permute-start.11) | collective-permute-done | bytes 262176 | tf_op jit(solution)/shard_map/ppermute | solution.py:207
  323.5 4.9 %collective-permute-done.10 = bf16[256,512]{1,0:T(8,128)(2,1)} collective-permute-done((bf16[256,512]{1,0:T(8,128)(2,1)}, bf16[256,512]{1,0:T(8,128)(2,1)}, u32[]{:S(2)}, u32[]{:S(2)}) %collective-permute-start.10) | collective-permute-done | bytes 262176 | tf_op jit(solution)/shard_map/ppermute | solution.py:207
  328.5 5.0 %collective-permute-done.9 = bf16[256,512]{1,0:T(8,128)(2,1)} collective-permute-done((bf16[256,512]{1,0:T(8,128)(2,1)}, bf16[256,512]{1,0:T(8,128)(2,1)}, u32[]{:S(2)}, u32[]{:S(2)}) %collective-permute-start.9) | collective-permute-done | bytes 262176 | tf_op jit(solution)/shard_map/ppermute | solution.py:207
  333.5 4.2 %collective-permute-done.7 = bf16[256,512]{1,0:T(8,128)(2,1)} collective-permute-done((bf16[256,512]{1,0:T(8,128)(2,1)S(1)}, bf16[256,512]{1,0:T(8,128)(2,1)}, u32[]{:S(2)}, u32[]{:S(2)}) %collective-permute-start.7) | collective-permute-done | bytes 262176 | tf_op jit(solution)/shard_map/ppermute | solution.py:207
  337.6 5.5 %collective-permute-done.6 = bf16[256,512]{1,0:T(8,128)(2,1)} collective-permute-done((bf16[256,512]{1,0:T(8,128)(2,1)S(1)}, bf16[256,512]{1,0:T(8,128)(2,1)}, u32[]{:S(2)}, u32[]{:S(2)}) %collective-permute-start.6) | collective-permute-done | bytes 262176 | tf_op jit(solution)/shard_map/ppermute | solution.py:207
  347.5 3.7 %collective-permute-done.3 = bf16[256,256]{1,0:T(8,128)(2,1)S(1)} collective-permute-done((bf16[256,256]{1,0:T(8,128)(2,1)S(1)}, bf16[256,256]{1,0:T(8,128)(2,1)S(1)}, u32[]{:S(2)}, u32[]{:S(2)}) %collective-permute-start.3) | collective-permute-done | bytes 131104 | tf_op jit(solution)/shard_map/ppermute | solution.py:172
  (62 shorter events, 25.2 us)
Async XLA Ops:
  7.2 30.5 %copy-start = (bf16[1,1024,1024]{2,1,0:T(8,128)(2,1)S(1)}, bf16[1,1024,1024]{2,1,0:T(8,128)(2,1)}, u32[]{:S(2)}) copy-start(bf16[1,1024,1024]{2,1,0:T(8,128)(2,1)} %param.8) | copy-start | bytes 6291460
  7.2 53.2 %all-gather.9.cloned.1.call-start = ((), (), s32[]{:S(2)}) async-start(), calls=%async_computation.8 | async-start | bytes 5242880 | tf_op jit(solution)/shard_map/all_gather | solution.py:228
  7.9 97.6 %all-gather.5.cloned.1.call-start = ((), (), s32[]{:S(2)}) async-start(), calls=%async_computation.3 | async-start | bytes 6684672 | tf_op jit(solution)/shard_map/all_gather | solution.py:224
  9.8 146.5 %all-gather.7.cloned.1.call-start = ((), (), s32[]{:S(2)}) async-start(), calls=%async_computation.4 | async-start | bytes 5242880 | tf_op jit(solution)/shard_map/all_gather | solution.py:229
  9.8 26.7 %collective-permute-start = (bf16[128,4096]{1,0:T(8,128)(2,1)}, bf16[128,4096]{1,0:T(8,128)(2,1)S(1)}, u32[]{:S(2)}, u32[]{:S(2)}) collective-permute-start(bf16[128,4096]{1,0:T(8,128)(2,1)} %bitcast.78), channel_id=1, source_target_pairs={{0,1},{1,0},{2,3},{3,2},{4,5},{5,4},{6,7},{7,6},{8,9},{9,8},{10,11... | collective-permute-start | bytes 3145736 | tf_op jit(solution)/shard_map/ppermute | solution.py:172
  36.6 1.0 copy-start.9
  37.6 168.1 %reduce-scatter.4.cloned.1.call-start = ((), (), s32[]{:S(2)}) async-start(), calls=%async_computation.5 | async-start | bytes 5242880 | tf_op jit(solution)/shard_map/reduce_scatter | solution.py:239
  37.6 9.2 %copy-start.1 = (bf16[1,1024,1024]{2,1,0:T(8,128)(2,1)S(1)}, bf16[1,1024,1024]{2,1,0:T(8,128)(2,1)}, u32[]{:S(2)}) copy-start(bf16[1,1024,1024]{2,1,0:T(8,128)(2,1)} %param.8) | copy-start | bytes 6291460
  37.6 1.1 copy-start.4
  38.7 1.0 copy-start.5
  114.8 139.8 %reduce-scatter.8.cloned.1.call-start = ((), (), s32[]{:S(2)}) async-start(), calls=%async_computation.7 | async-start | bytes 5242880 | tf_op jit(solution)/shard_map/reduce_scatter | solution.py:239
  124.3 220.5 %reduce-scatter.6.cloned.1.call-start = ((), (), s32[]{:S(2)}) async-start(), calls=%async_computation.6 | async-start | bytes 1310720 | tf_op jit(solution)/shard_map/reduce_scatter | solution.py:187
  207.5 51.4 %collective-permute-start.1 = (bf16[1024,256]{1,0:T(8,128)(2,1)}, bf16[1024,256]{1,0:T(8,128)(2,1)S(1)}, u32[]{:S(2)}, u32[]{:S(2)}) collective-permute-start(bf16[1024,256]{1,0:T(8,128)(2,1)} %dynamic-slice_bitcast_fusion.3), channel_id=1, source_target_pairs={{0,1},{1,0},{2,3},{3,2},{4,5},{5,4},{6,7},{7,6},{8,9},{9,8},{10,11... | collective-permute-start | bytes 1572872 | tf_op jit(solution)/shard_map/ppermute | solution.py:172
  210.5 48.4 %copy-start.2 = (bf16[2,1024,256]{2,1,0:T(8,128)(2,1)S(1)}, bf16[2,1024,256]{2,1,0:T(8,128)(2,1)}, u32[]{:S(2)}) copy-start(bf16[2,1024,256]{2,1,0:T(8,128)(2,1)} %reduce-scatter.4.cloned.1.call-done.refs_4_) | copy-start | bytes 3145732
  255.7 20.8 %collective-permute-start.4 = (bf16[1024,256]{1,0:T(8,128)(2,1)S(1)}, bf16[1024,256]{1,0:T(8,128)(2,1)S(1)}, u32[]{:S(2)}, u32[]{:S(2)}) collective-permute-start(bf16[1024,256]{1,0:T(8,128)(2,1)S(1)} %dynamic-slice_bitcast_fusion.2), channel_id=1, source_target_pairs={{0,1},{1,0},{2,3},{3,2},{4,5},{5,4},{6,7},{7,6},{8,9},{9,8},{10,11... | collective-permute-start | bytes 1572872 | tf_op jit(solution)/shard_map/ppermute | solution.py:172
  259.0 29.5 %slice-start = ((s8[8388608]{0:T(1024)(128)(4,1)}), s8[4194304]{0:T(1024)(128)(4,1)S(1)}, s32[]{:S(2)}) async-start(s8[8388608]{0:T(1024)(128)(4,1)} %bitcast.67), calls=%async_computation.9 | async-start | bytes 8388608
  270.0 7.4 %copy-start.3 = (bf16[2,1024,256]{2,1,0:T(8,128)(2,1)S(1)}, bf16[2,1024,256]{2,1,0:T(8,128)(2,1)}, u32[]{:S(2)}) copy-start(bf16[2,1024,256]{2,1,0:T(8,128)(2,1)} %reduce-scatter.8.cloned.1.call-done.refs_4_) | copy-start | bytes 3145732
  270.0 18.4 %slice-start.1 = ((s8[8388608]{0:T(1024)(128)(4,1)}), s8[4194304]{0:T(1024)(128)(4,1)S(1)}, s32[]{:S(2)}) async-start(s8[8388608]{0:T(1024)(128)(4,1)} %bitcast.67), calls=%async_computation.10 | async-start | bytes 8388608
  276.1 1.4 copy-start.7
  276.2 20.8 %collective-permute-start.2 = (bf16[8,256,256]{2,1,0:T(8,128)(2,1)S(1)}, bf16[8,256,256]{2,1,0:T(8,128)(2,1)}, u32[]{:S(2)}, u32[]{:S(2)}) collective-permute-start(bf16[8,256,256]{2,1,0:T(8,128)(2,1)S(1)} %dynamic-slice_bitcast_fusion.1), channel_id=1, source_target_pairs={{0,8},{8,0},{1,9},{9,1},{2,10},{10,2},{3,11},{11,3},{4,12},{12,4},... | collective-permute-start | bytes 3145736 | tf_op jit(solution)/shard_map/ppermute | solution.py:172
  293.3 2.1 copy-start.6
  293.3 3.7 %copy-start.8 = (bf16[4096,256]{1,0:T(8,128)(2,1)S(1)}, bf16[4096,256]{1,0:T(8,128)(2,1)}, u32[]{:S(2)}) copy-start(bf16[4096,256]{1,0:T(8,128)(2,1)} %copy-done.7) | copy-start | bytes 6291460
  297.0 4.5 %collective-permute-start.5 = (bf16[8,256,512]{2,1,0:T(8,128)(2,1)}, bf16[8,256,512]{2,1,0:T(8,128)(2,1)}, u32[]{:S(2)}, u32[]{:S(2)}) collective-permute-start(bf16[8,256,512]{2,1,0:T(8,128)(2,1)} %dynamic-slice_bitcast_fusion), channel_id=1, source_target_pairs={{0,8},{8,0},{1,9},{9,1},{2,10},{10,2},{3,11},{11,3},{4,12},{12,4},... | collective-permute-start | bytes 6291464 | tf_op jit(solution)/shard_map/ppermute | solution.py:172
  305.3 10.1 %collective-permute-start.12 = (bf16[256,512]{1,0:T(8,128)(2,1)S(1)}, bf16[256,512]{1,0:T(8,128)(2,1)S(1)}, u32[]{:S(2)}, u32[]{:S(2)}) collective-permute-start(bf16[256,512]{1,0:T(8,128)(2,1)S(1)} %get-tuple-element.20), channel_id=1, source_target_pairs={{0,112},{16,64},{32,80},{48,96},{64,48},{80,0},{96,16},{112,32},{1... | collective-permute-start | bytes 786440 | tf_op jit(solution)/shard_map/ppermute | solution.py:207
  308.3 14.4 %collective-permute-start.11 = (bf16[256,512]{1,0:T(8,128)(2,1)S(1)}, bf16[256,512]{1,0:T(8,128)(2,1)S(1)}, u32[]{:S(2)}, u32[]{:S(2)}) collective-permute-start(bf16[256,512]{1,0:T(8,128)(2,1)S(1)} %get-tuple-element.21), channel_id=1, source_target_pairs={{0,96},{16,112},{32,64},{48,80},{64,32},{80,48},{96,0},{112,16},{1... | collective-permute-start | bytes 786440 | tf_op jit(solution)/shard_map/ppermute | solution.py:207
  309.8 18.7 %collective-permute-start.10 = (bf16[256,512]{1,0:T(8,128)(2,1)}, bf16[256,512]{1,0:T(8,128)(2,1)}, u32[]{:S(2)}, u32[]{:S(2)}) collective-permute-start(bf16[256,512]{1,0:T(8,128)(2,1)} %get-tuple-element.22), channel_id=1, source_target_pairs={{0,80},{16,96},{32,112},{48,64},{64,16},{80,32},{96,48},{112,0},{1... | collective-permute-start | bytes 786440 | tf_op jit(solution)/shard_map/ppermute | solution.py:207
  310.8 22.7 %collective-permute-start.9 = (bf16[256,512]{1,0:T(8,128)(2,1)}, bf16[256,512]{1,0:T(8,128)(2,1)}, u32[]{:S(2)}, u32[]{:S(2)}) collective-permute-start(bf16[256,512]{1,0:T(8,128)(2,1)} %get-tuple-element.23), channel_id=1, source_target_pairs={{0,64},{16,80},{32,96},{48,112},{64,0},{80,16},{96,32},{112,48},{1... | collective-permute-start | bytes 786440 | tf_op jit(solution)/shard_map/ppermute | solution.py:207
  312.2 21.3 %collective-permute-start.8 = (bf16[256,512]{1,0:T(8,128)(2,1)S(1)}, bf16[256,512]{1,0:T(8,128)(2,1)}, u32[]{:S(2)}, u32[]{:S(2)}) collective-permute-start(bf16[256,512]{1,0:T(8,128)(2,1)S(1)} %get-tuple-element.24), channel_id=1, source_target_pairs={{0,48},{16,0},{32,16},{48,32},{64,112},{80,64},{96,80},{112,96},{1... | collective-permute-start | bytes 786440 | tf_op jit(solution)/shard_map/ppermute | solution.py:207
  315.4 22.2 %collective-permute-start.7 = (bf16[256,512]{1,0:T(8,128)(2,1)S(1)}, bf16[256,512]{1,0:T(8,128)(2,1)}, u32[]{:S(2)}, u32[]{:S(2)}) collective-permute-start(bf16[256,512]{1,0:T(8,128)(2,1)S(1)} %get-tuple-element.25), channel_id=1, source_target_pairs={{0,32},{16,48},{32,0},{48,16},{64,96},{80,112},{96,64},{112,80},{1... | collective-permute-start | bytes 786440 | tf_op jit(solution)/shard_map/ppermute | solution.py:207
  322.7 20.5 %collective-permute-start.6 = (bf16[256,512]{1,0:T(8,128)(2,1)S(1)}, bf16[256,512]{1,0:T(8,128)(2,1)}, u32[]{:S(2)}, u32[]{:S(2)}) collective-permute-start(bf16[256,512]{1,0:T(8,128)(2,1)S(1)} %get-tuple-element.19), channel_id=1, source_target_pairs={{0,16},{16,32},{32,48},{48,0},{64,80},{80,96},{96,112},{112,64},{1... | collective-permute-start | bytes 786440 | tf_op jit(solution)/shard_map/ppermute | solution.py:207
  345.7 5.5 %collective-permute-start.3 = (bf16[256,256]{1,0:T(8,128)(2,1)S(1)}, bf16[256,256]{1,0:T(8,128)(2,1)S(1)}, u32[]{:S(2)}, u32[]{:S(2)}) collective-permute-start(bf16[256,256]{1,0:T(8,128)(2,1)S(1)} %dynamic-slice_bitcast_fusion.11), channel_id=1, source_target_pairs={{0,64},{64,0},{1,65},{65,1},{2,66},{66,2},{3,67},{67,3},{4,68},{68... | collective-permute-start | bytes 393224 | tf_op jit(solution)/shard_map/ppermute | solution.py:172
Sparse Core Ops, SparseCore 0:
  9.7 50.6 all-gather.8
  62.7 42.7 all-gather.4
  107.2 49.0 all-gather.6
  158.5 47.1 reduce-scatter.3
  208.0 46.5 reduce-scatter.7
  299.7 40.2 reduce-scatter.5

commit v2 on v1

v2 whole, which is shorter than its diff:
```python
import jax
import jax.numpy as jnp
from jax import lax
from jax.experimental import pallas as pl
from jax.experimental.pallas import tpu as pltpu
from jax.sharding import Mesh, PartitionSpec as P

HEAD = 128
FACTOR = HEAD ** (-0.5)
LOG2E = 1.4426950408889634
BLOCK = 256
SEQ = 1024
DP = ("ylo", "z", "core")
TENSOR = ("x", "yhi")
NT = (((1,), (1,)), ((), ()))
VMEM = pltpu.CompilerParams(vmem_limit_bytes=48 * 1024 * 1024)


def cost(us, moved=0):
    return pl.CostEstimate(flops=int(us * 1.0e9), bytes_accessed=moved, transcendentals=0)


def dot(a, b):
    return jnp.dot(a, b, preferred_element_type=jnp.float32)


def teacher_kernel(q_ref, k_ref, v_ref, o_ref):
    for number in range(SEQ // BLOCK):
        first = number * BLOCK
        limit = first + BLOCK
        scores = lax.dot_general(
            q_ref[first:limit, :], k_ref[:limit, :], NT, preferred_element_type=jnp.float32
        )
        row = lax.broadcasted_iota(jnp.int32, (BLOCK, BLOCK), 0)
        col = lax.broadcasted_iota(jnp.int32, (BLOCK, BLOCK), 1)
        last = jnp.where(col <= row, scores[:, first:], -1e30)
        scores = jnp.concatenate([scores[:, :first], last], axis=1) if first else last
        top = jnp.max(scores, axis=1, keepdims=True)
        weights = jnp.exp2((scores - top) * (FACTOR * LOG2E))
        total = jnp.sum(weights, axis=1, keepdims=True)
        context = dot(weights.astype(jnp.bfloat16), v_ref[:limit, :])
        o_ref[first:limit, :] = (context / total).astype(jnp.bfloat16)


def teacher_attention(queries, keys, values, first, count):
    return pl.pallas_call(
        teacher_kernel,
        grid=(count,),
        in_specs=[
            pl.BlockSpec((SEQ, HEAD), lambda h: (0, first + h)),
            pl.BlockSpec((SEQ, HEAD), lambda h: (0, 0)),
            pl.BlockSpec((SEQ, HEAD), lambda h: (0, 0)),
        ],
        out_specs=pl.BlockSpec((SEQ, HEAD), lambda h: (0, h)),
        out_shape=jax.ShapeDtypeStruct((SEQ, count * HEAD), jnp.bfloat16),
        compiler_params=VMEM,
        cost_estimate=cost(7),
        name="teacher_attention",
    )(queries, keys, values)


def project_kernel(order_ref, a_ref, b_ref, p_ref, o_ref, context):
    half = a_ref.shape[1]

    @pl.when(pl.program_id(0) == 0)
    def _():
        context[:, :half] = a_ref[...]
        context[:, half:] = b_ref[...]

    o_ref[0] = dot(context[...], p_ref[...]).astype(jnp.bfloat16)


def project(order, context_a, context_b, projector):
    rows = projector.shape[0]
    count = order.shape[0]
    return pl.pallas_call(
        project_kernel,
        grid_spec=pltpu.PrefetchScalarGridSpec(
            num_scalar_prefetch=1,
            grid=(count,),
            in_specs=[
                pl.BlockSpec(context_a.shape, lambda g, order: (0, 0)),
                pl.BlockSpec(context_b.shape, lambda g, order: (0, 0)),
                pl.BlockSpec((rows, 256), lambda g, order: (0, order[g])),
            ],
            out_specs=pl.BlockSpec((1, SEQ, 256), lambda g, order: (g, 0, 0)),
            scratch_shapes=[pltpu.VMEM((SEQ, rows), jnp.bfloat16)],
        ),
        out_shape=jax.ShapeDtypeStruct((count, SEQ, 256), jnp.bfloat16),
        compiler_params=VMEM,
        cost_estimate=cost(count),
        name="project",
    )(order, context_a, context_b, projector)


def fill(scratch, piece_refs):
    at = 0
    for ref in piece_refs:
        scratch[at : at + ref.shape[0], :] = ref[...]
        at += ref.shape[0]


def student_project_kernel(*refs):
    at_ref, pieces, (w_ref, o_ref, left, total) = refs[0], refs[1:-4], refs[-4:]
    step = pl.program_id(0)
    fill(left, pieces)
    product = dot(left[...], w_ref[...])

    @pl.when(step == 0)
    def _():
        total[...] = product

    @pl.when(step > 0)
    def _():
        total[...] += product

    @pl.when(step == pl.num_programs(0) - 1)
    def _():
        first = 0
        for number, ref in enumerate(pieces):
            size = ref.shape[0]
            o_ref[pl.ds(pl.multiple_of(at_ref[number], 64), size), :] = total[
                first : first + size, :
            ].astype(jnp.bfloat16)
            first += size


def student_project(places, pieces, weights):
    depth, cols = weights.shape
    block = 1024
    return pl.pallas_call(
        student_project_kernel,
        grid_spec=pltpu.PrefetchScalarGridSpec(
            num_scalar_prefetch=1,
            grid=(depth // block,),
            in_specs=[pl.BlockSpec((p.shape[0], block), lambda k, at: (0, k)) for p in pieces]
            + [pl.BlockSpec((block, cols), lambda k, at: (k, 0))],
            out_specs=pl.BlockSpec((SEQ, cols), lambda k, at: (0, 0)),
            scratch_shapes=[
                pltpu.VMEM((SEQ, block), jnp.bfloat16),
                pltpu.VMEM((SEQ, cols), jnp.float32),
            ],
        ),
        out_shape=jax.ShapeDtypeStruct((SEQ, cols), jnp.bfloat16),
        compiler_params=VMEM,
        cost_estimate=cost(9),
        name="student_project",
    )(places, *pieces, weights)


def weight_grad_kernel(count, *refs):
    at_ref, grads, pieces = refs[0], refs[2 : 2 + count], refs[2 + count : -4]
    o_ref, left, right, across = refs[-4:]

    @pl.when(pl.program_id(0) == 0)
    def _():
        first = 0
        for number, ref in enumerate(pieces):
            size = ref.shape[0]
            col = 0
            for grad in grads:
                right[first : first + size, col : col + grad.shape[1]] = grad[
                    pl.ds(pl.multiple_of(at_ref[number], 64), size), :
                ]
                col += grad.shape[1]
            first += size
        across[...] = right[...].T

    fill(left, pieces)
    o_ref[0] = dot(across[...], left[...]).astype(jnp.bfloat16)


def weight_grad(places, blocks, grads, pieces):
    cols = sum(g.shape[1] for g in grads)
    return pl.pallas_call(
        lambda *refs: weight_grad_kernel(len(grads), *refs),
        grid_spec=pltpu.PrefetchScalarGridSpec(
            num_scalar_prefetch=2,
            grid=(8,),
            in_specs=[pl.BlockSpec(g.shape, lambda k, at, order: (0, 0)) for g in grads]
            + [
                pl.BlockSpec((p.shape[0], 256), lambda k, at, order: (0, order[k])) for p in pieces
            ],
            out_specs=pl.BlockSpec((1, cols, 256), lambda k, at, order: (k, 0, 0)),
            scratch_shapes=[
                pltpu.VMEM((SEQ, 256), jnp.bfloat16),
                pltpu.VMEM((SEQ, cols), jnp.bfloat16),
                pltpu.VMEM((cols, SEQ), jnp.bfloat16),
            ],
        ),
        out_shape=jax.ShapeDtypeStruct((8, cols, 256), jnp.bfloat16),
        compiler_params=VMEM,
        cost_estimate=cost(4),
        name="weight_grad",
    )(places, blocks, *grads, *pieces)


def pair_kernel(a_ref, b_ref, *outs):
    for number, ref in enumerate(outs):
        ref[...] = (
            a_ref[number].astype(jnp.float32) + b_ref[number].astype(jnp.float32)
        ).astype(jnp.bfloat16)


def pair_sum(a, b):
    return pl.pallas_call(
        pair_kernel,
        out_shape=[jax.ShapeDtypeStruct(a.shape[1:], jnp.bfloat16) for _ in range(a.shape[0])],
        compiler_params=VMEM,
        cost_estimate=cost(3),
        name="pair_sum",
    )(a, b)


def student_kernel(has_start, y_ref, q_ref, k_ref, v_ref, mine_ref, *rest):
    if has_start:
        start_ref, gq_ref, gkv_ref, kt, vt, dk, dv = rest
    else:
        theirs_ref, gq_ref, gkv_ref, kt, vt, dk, dv = rest
    step = pl.program_id(0)

    @pl.when(step == 0)
    def _():
        kt[...] = k_ref[...].T
        vt[...] = v_ref[...].T
        if has_start:
            dk[...] = start_ref[:, :HEAD]
            dv[...] = start_ref[:, HEAD:]
        else:
            dk[...] = jnp.zeros_like(dk)
            dv[...] = jnp.zeros_like(dv)

    for number in range(SEQ // BLOCK):
        first = number * BLOCK
        limit = first + BLOCK
        queries = q_ref[first:limit, :]
        scores = lax.dot_general(k_ref[:limit, :], queries, NT, preferred_element_type=jnp.float32)
        key = lax.broadcasted_iota(jnp.int32, (BLOCK, BLOCK), 0)
        query = lax.broadcasted_iota(jnp.int32, (BLOCK, BLOCK), 1)
        last = jnp.where(key <= query, scores[first:], -1e30)
        scores = jnp.concatenate([scores[:first], last], axis=0) if first else last
        top = jnp.max(scores, axis=0, keepdims=True)
        weights = jnp.exp2((scores - top) * (FACTOR * LOG2E))
        probs = weights * (1.0 / jnp.sum(weights, axis=0, keepdims=True))
        rounded = probs.astype(jnp.bfloat16)
        context = dot(vt[:, :limit], rounded).T
        target = mine_ref[0, first:limit, :].astype(jnp.float32)
        if not has_start:
            target += theirs_ref[first:limit, :].astype(jnp.float32)
        incoming = ((context - target) * (1.0 / 16)).astype(jnp.bfloat16)
        grad_probs = lax.dot_general(
            v_ref[:limit, :], incoming, NT, preferred_element_type=jnp.float32
        )
        inner = jnp.sum(grad_probs * probs, axis=0, keepdims=True)
        scaled = (probs * (grad_probs - inner)).astype(jnp.bfloat16)
        dv[:limit, :] += dot(rounded, incoming)
        dk[:limit, :] += dot(scaled, queries)
        gq_ref[first:limit, :] = (dot(kt[:, :limit], scaled) * FACTOR).T.astype(jnp.bfloat16)

    @pl.when(step == pl.num_programs(0) - 1)
    def _():
        keys_scale = 1.0 if gkv_ref.dtype == jnp.float32 else FACTOR
        gkv_ref[:, :HEAD] = (dk[...] * keys_scale).astype(gkv_ref.dtype)
        gkv_ref[:, HEAD:] = dv[...].astype(gkv_ref.dtype)


def student_attention(y, projected, mine, part, theirs=None, start=None):
    specs = [
        pl.BlockSpec((SEQ, HEAD), lambda h, y: (0, 2 * part + h)),
        pl.BlockSpec((SEQ, HEAD), lambda h, y: (0, 4)),
        pl.BlockSpec((SEQ, HEAD), lambda h, y: (0, 5)),
        pl.BlockSpec((1, SEQ, HEAD), lambda h, y: (y[0], 0, h)),
    ]
    operands = [projected, projected, projected, mine]
    if theirs is not None:
        specs.append(pl.BlockSpec((SEQ, HEAD), lambda h, y: (0, h)))
        operands.append(theirs)
    if start is not None:
        specs.append(pl.BlockSpec((SEQ, 2 * HEAD), lambda h, y: (0, 0)))
        operands.append(start)
    return pl.pallas_call(
        lambda *refs: student_kernel(start is not None, *refs),
        grid_spec=pltpu.PrefetchScalarGridSpec(
            num_scalar_prefetch=1,
            grid=(2,),
            in_specs=specs,
            out_specs=[
                pl.BlockSpec((SEQ, HEAD), lambda h, y: (0, h)),
                pl.BlockSpec((SEQ, 2 * HEAD), lambda h, y: (0, 0)),
            ],
            scratch_shapes=[
                pltpu.VMEM((HEAD, SEQ), jnp.bfloat16),
                pltpu.VMEM((HEAD, SEQ), jnp.bfloat16),
                pltpu.VMEM((SEQ, HEAD), jnp.float32),
                pltpu.VMEM((SEQ, HEAD), jnp.float32),
            ],
        ),
        out_shape=[
            jax.ShapeDtypeStruct((SEQ, 2 * HEAD), jnp.bfloat16),
            jax.ShapeDtypeStruct(
                (SEQ, 2 * HEAD), jnp.float32 if start is None else jnp.bfloat16
            ),
        ],
        compiler_params=VMEM,
        cost_estimate=cost(11),
        name="student_attention",
    )(y, *operands)


def shift(array, axis, step=1):
    n = lax.axis_size(axis)
    return lax.ppermute(array, axis, [(i, (i + step) % n) for i in range(n)])


def gather_rows_near(own):
    return shift(own, "yhi"), shift(own, "x", 1), shift(own, "x", -1)


def far_halves(left, right):
    half = left.shape[0] // 2
    return shift(left[:half], "x", 1), shift(right[half:], "x", -1)


def row_places(x, y):
    places = []
    for side in (y, 1 - y):
        for dx, offset in ((0, 0), (3, 0), (1, 0), (2, 0), (2, 64)):
            places.append((((x + dx) % 4) * 2 + side) * 128 + offset)
    return jnp.stack(places).astype(jnp.int32)


RELATIVE = [(dy, dz) for dy in range(2) for dz in range(4)]


def row_blocks(core):
    y = lax.axis_index("ylo")
    z = lax.axis_index("z")
    return jnp.stack(
        [(((y + dy) % 2) * 4 + (z + dz) % 4) * 2 + core for dy, dz in RELATIVE]
    ).astype(jnp.int32)


def send_direct(blocks):
    got = [blocks[0]]
    for (dy, dz), block in zip(RELATIVE[1:], blocks[1:]):
        route = [(i * 4 + k, (i + dy) % 2 * 4 + (k + dz) % 4) for i in range(2) for k in range(4)]
        got.append(lax.ppermute(block, ("ylo", "z"), route))
    return got


def finish_kernel(*refs):
    a_refs, b_refs, (q_ref, k_ref, v_ref) = refs[:8], refs[8:16], refs[16:]

    def total(parts):
        result = parts[0][...].astype(jnp.float32)
        for part in parts[1:]:
            result += part[...].astype(jnp.float32)
        return result.T

    q_ref[:, :256] = total(a_refs)
    rest = total(b_refs)
    q_ref[:, 256:] = rest[:, :256]
    k_ref[...] = rest[:, 256:384]
    v_ref[...] = rest[:, 384:]


def finish(got_a, got_b):
    return pl.pallas_call(
        finish_kernel,
        out_shape=[jax.ShapeDtypeStruct((256, cols), jnp.float32) for cols in (512, 128, 128)],
        compiler_params=VMEM,
        cost_estimate=cost(3),
        name="finish",
    )(*got_a, *got_b)


def per_device(
    teacher_queries,
    teacher_keys,
    teacher_values,
    projector,
    student_inputs,
    query_weight,
    key_weight,
    value_weight,
):
    tq, tk, tv = teacher_queries[0], teacher_keys[0], teacher_values[0]
    x = lax.axis_index("x")
    yhi = lax.axis_index("yhi")
    core = lax.axis_index("core")
    own = student_inputs[0]
    weights = lax.all_gather(
        jnp.concatenate([query_weight, key_weight, value_weight], axis=1), DP, axis=0, tiled=True
    )
    other, left, right = gather_rows_near(own)

    groups = jnp.arange(4, dtype=jnp.int32)
    context_a = teacher_attention(tq, tk, tv, 0, 4)
    context_b = teacher_attention(tq, tk, tv, 4, 4)
    far = far_halves(left, right)
    context_b, far, other, weights = lax.optimization_barrier((context_b, far, other, weights))

    other_left, other_right = shift(other, "x", 1), shift(other, "x", -1)

    product_a = project(2 * jnp.arange(8, dtype=jnp.int32), context_a, context_b, projector)
    sum_a = lax.psum_scatter(product_a, "x", scatter_dimension=0, tiled=True)

    sent = project(2 * (2 * groups + 1 - yhi) + 1, context_a, context_b, projector)
    came = shift(sent, "yhi")
    context_b, other_left, other_right = lax.optimization_barrier(
        (context_b, other_left, other_right)
    )
    kept = project(2 * (2 * groups + yhi) + 1, context_a, context_b, projector)

    other_far = far_halves(other_left, other_right)
    pieces = [own, left, right, *far, other, other_left, other_right, *other_far]
    places = row_places(x, yhi)
    projected = student_project(places, pieces, weights)

    both = (kept.astype(jnp.float32) + came.astype(jnp.float32)).astype(jnp.bfloat16)
    sum_b = lax.psum_scatter(both, "x", scatter_dimension=0, tiled=True)

    y = yhi.astype(jnp.int32).reshape(1)
    theirs_a = shift(lax.dynamic_index_in_dim(sum_a, 1 - yhi, 0, keepdims=False), "yhi")

    def reduced(grads):
        sent = weight_grad(places, row_blocks(1 - core), grads, pieces)
        kept = weight_grad(places, row_blocks(core), grads, pieces)
        return list(pair_sum(kept, shift(sent, "core")))

    grad_a, part_kv = student_attention(y, projected, sum_a, 0, theirs=theirs_a)
    blocks_a = reduced([grad_a])
    sum_b, blocks_a[0] = lax.optimization_barrier((sum_b, blocks_a[0]))
    got_a = send_direct(blocks_a)
    grad_b, grad_kv = student_attention(
        jnp.zeros((1,), jnp.int32), projected, sum_b, 1, start=part_kv
    )
    got_a, grad_b = lax.optimization_barrier((got_a, grad_b))
    got_b = send_direct(reduced([grad_b, grad_kv]))
    return tuple(finish(got_a, got_b))


def solution(mesh):
    fine = Mesh(mesh.devices.reshape(2, 4, 2, 4, 2), DP + TENSOR)
    placed = (
        P(DP, None, TENSOR),
        P(DP, None, TENSOR),
        P(DP, None, TENSOR),
        P(TENSOR, None),
        P(DP, TENSOR, None),
        P(DP, TENSOR),
        P(DP, TENSOR),
        P(DP, TENSOR),
    )
    return jax.shard_map(
        per_device,
        mesh=fine,
        in_specs=placed,
        out_specs=(P(DP, TENSOR), P(DP, TENSOR), P(DP, TENSOR)),
        check_vma=False,
    )
```

time: 361 us -> 310 us (0.86); the launches traced: 360 us -> 305 us
  waiting for transfers between devices: 210 us -> 114 us
  Pallas kernels: 55 us -> 103 us
  matrix products: 21.8 us -> 0 us
  local copies, waits for them, and re-layouts: 14.4 us -> 31.1 us
  other arithmetic: 20.2 us -> 3.85 us
  starting transfers between devices: 24.5 us -> 37.8 us
    reduce_scatter x3 -> x2, waiting for transfers between devices: 71.8 us -> 4.53 us  [the longest x1 4.53 us: per_device(): sum_a = lax.psum_scatter(product_a, 'x', scatter_dimension=0, tiled=True)]
    pallas_call x2 -> x11, Pallas kernels: 18.7 us -> 67.5 us  [the longest x4 30.9 us: weight_grad(): pl.pallas_call(lambda *refs: weight_grad_kernel(len(grads), *refs), grid_...]
    all_gather x2 -> x0, waiting for transfers between devices: 38.3 us -> none  [the longest x1 31.9 us: per_device(): other_all = lax.all_gather(other, 'x', axis=0, tiled=True)]
    ppermute x6 -> x13, waiting for transfers between devices: 28.9 us -> 64.7 us  [shift(): return lax.ppermute(array, axis, [(i, (i + step) % n) for i in range(n)])]
    all_gather x1, waiting for transfers between devices: 45.1 us -> 11.2 us  [per_device(): lax.all_gather(jnp.concatenate([query_weight, key_weight, value_weight],...]
    unnamed x24 -> x82, local copies, waits for them, and re-layouts: 6.13 us -> 27.9 us
    dot_general x3 -> x0, matrix products: 21.8 us -> none  [the longest x1 11 us: dot(): return jnp.dot(a, b, preferred_element_type=jnp.float32)]
    select_n x1 -> x0, other arithmetic: 10.7 us -> none  [per_device(): rows_all = jnp.where(yhi == 0, pieces, flipped).reshape(SEQ, -1)]
  transfers between devices with their start and end apart: 19 -> 30, of which waited for: 14 -> 9; matrix products, arithmetic and copies ran while one was open for 13% -> 2% of each run, Pallas kernels for 15% -> 27%
where the time goes in v2:
time: 310 us; the launch traced here: 305 us
  waiting for transfers between devices  114 us (37%)
  Pallas kernels  103 us (33%)
  starting transfers between devices  37.8 us (12%)
  local copies, waits for them, and re-layouts  31.1 us (10%)
  between operations  14.2 us (5%)
  other arithmetic  3.85 us (1%)
    ppermute x13, waiting for transfers between devices, shift(): return lax.ppermute(array, axis, [(i, (i + step) % n) for i in range(n)])  64.7 us
    ppermute x14, waiting for transfers between devices, send_direct(): got.append(lax.ppermute(block, ('ylo', 'z'), route))  34 us
    pallas_call x4, Pallas kernels, weight_grad(): pl.pallas_call(lambda *refs: weight_grad_kernel(len(grads), *refs), grid_...  30.9 us
    unnamed x82, local copies, waits for them, and re-layouts  27.9 us
    pallas_call x2, Pallas kernels, student_attention(): pl.pallas_call(lambda *refs: student_kernel(start is not None, *refs), gr...  21.6 us
    ppermute x13, starting transfers between devices, shift(): return lax.ppermute(array, axis, [(i, (i + step) % n) for i in range(n)])  21.6 us
    pallas_call x3, Pallas kernels, project(): pl.pallas_call(project_kernel, grid_spec=pltpu.PrefetchScalarGridSpec(num...  20 us
    ppermute x14, starting transfers between devices, send_direct(): got.append(lax.ppermute(block, ('ylo', 'z'), route))  16 us
  transfers between devices with their start and end apart: 30, of which 9 were waited for; matrix products, arithmetic and copies ran while one was open for 2% of the time, Pallas kernels for 27%

profile of v2, /device:TPU:0, one launch (start us, length us, event | category | flops | bytes accessed | tf_op | source)
XLA Modules:
  0.0 304.9 jit_solution(5029559545257396872)
XLA Ops:
  7.2 1.8 pad_maximum_fusion
  12.4 3.3 %collective-permute-start.4 = (bf16[128,4096]{1,0:T(8,128)(2,1)}, bf16[128,4096]{1,0:T(8,128)(2,1)S(1)}, u32[]{:S(2)}, u32[]{:S(2)}) collective-permute-start(bf16[128,4096]{1,0:T(8,128)(2,1)} %bitcast.37), channel_id=1, source_target_pairs={{0,1},{1,0},{2,3},{3,2},{4,5},{5,4},{6,7},{7,6},{8,9},{9,8},{10,11... | collective-permute-start | bytes 3145736 | tf_op jit(solution)/shard_map/ppermute | solution.py:312
  19.2 7.2 %teacher_attention.3.b_ref = bf16[1024,512]{1,0:T(8,128)(2,1)S(1)} custom-call(bf16[1024,1024]{1,0:T(8,128)(2,1)S(1)} %bitcast.33, bf16[1024,128]{1,0:T(8,128)(2,1)S(1)} %bitcast.43, bf16[1024,128]{1,0:T(8,128)(2,1)S(1)} %bitcast.45), custom_call_target="tpu_custom_call" | custom-call | flops 7000000000 | tf_op jit(solution)/shard_map/teacher_attention/pallas_call | solution.py:46
  26.4 9.0 %collective-permute-done.refs_2_.refs_4_.refs_5_ = bf16[128,4096]{1,0:T(8,128)(2,1)S(1)} collective-permute-done((bf16[128,4096]{1,0:T(8,128)(2,1)}, bf16[128,4096]{1,0:T(8,128)(2,1)S(1)}, u32[]{:S(2)}, u32[]{:S(2)}) %collective-permute-start) | collective-permute-done | bytes 1048608 | tf_op jit(solution)/shard_map/ppermute | solution.py:312
  36.0 2.8 collective-permute-start.3
  38.9 7.2 %teacher_attention.2.a_ref = bf16[1024,512]{1,0:T(8,128)(2,1)S(1)} custom-call(bf16[1024,1024]{1,0:T(8,128)(2,1)S(1)} %bitcast.34, bf16[1024,128]{1,0:T(8,128)(2,1)S(1)} %bitcast.44, bf16[1024,128]{1,0:T(8,128)(2,1)S(1)} %bitcast.46), custom_call_target="tpu_custom_call" | custom-call | flops 7000000000 | tf_op jit(solution)/shard_map/teacher_attention/pallas_call | solution.py:46
  47.0 9.2 %collective-permute-done.4.refs_6_.refs_8_.refs_9_ = bf16[128,4096]{1,0:T(8,128)(2,1)S(1)} collective-permute-done((bf16[128,4096]{1,0:T(8,128)(2,1)}, bf16[128,4096]{1,0:T(8,128)(2,1)S(1)}, u32[]{:S(2)}, u32[]{:S(2)}) %collective-permute-start.4) | collective-permute-done | bytes 1048608 | tf_op jit(solution)/shard_map/ppermute | solution.py:312
  58.8 11.2 %all-gather.2.cloned.1.call-done.refs_11_ = bf16[4096,768]{1,0:T(8,128)(2,1)} async-done(((bf16[256,768]{1,0:T(8,128)(2,1)}), bf16[4096,768]{1,0:T(8,128)(2,1)}) %all-gather.2.cloned.1.call-update) | async-done | bytes 6291472 | tf_op jit(solution)/shard_map/all_gather | solution.py:392
  71.2 10.0 %project.5 = bf16[8,1024,256]{2,1,0:T(8,128)(2,1)} custom-call(s32[8]{0:T(128)S(1)} %iota_multiply_fusion.order_ref, bf16[1024,512]{1,0:T(8,128)(2,1)S(1)} %copy-done.24, bf16[1024,512]{1,0:T(8,128)(2,1)S(1)} %teacher_attention.3.b_ref, bf16[1024,4096]{1,0:T(8,128)(2,1)} %p_ref.5), custom_call_target="tpu_custom_call" | custom-call | flops 8000000000 | tf_op jit(solution)/shard_map/project/pallas_call | solution.py:76
  82.5 5.0 %project.4 = bf16[4,1024,256]{2,1,0:T(8,128)(2,1)S(1)} custom-call(s32[4]{0:T(128)S(1)} %multiply_add_fusion.order_ref, bf16[1024,512]{1,0:T(8,128)(2,1)S(1)} %copy-done.25, bf16[1024,512]{1,0:T(8,128)(2,1)S(1)} %teacher_attention.3.b_ref, bf16[1024,4096]{1,0:T(8,128)(2,1)} %p_ref.5), custom_call_target="tpu_custom_call" | custom-call | flops 4000000000 | tf_op jit(solution)/shard_map/project/pallas_call | solution.py:76
  87.6 2.2 collective-permute-start.7
  90.4 2.6 collective-permute-start.6
  93.0 45.9 %collective-permute-done.5.refs_7_.refs_9_.refs_10_ = bf16[128,4096]{1,0:T(8,128)(2,1)S(1)} collective-permute-done((bf16[128,4096]{1,0:T(8,128)(2,1)S(1)}, bf16[128,4096]{1,0:T(8,128)(2,1)S(1)}, u32[]{:S(2)}, u32[]{:S(2)}) %collective-permute-start.5) | collective-permute-done | bytes 1048608 | tf_op jit(solution)/shard_map/ppermute | solution.py:312
  141.5 2.5 collective-permute-start.9
  144.0 5.0 %project.3 = bf16[4,1024,256]{2,1,0:T(8,128)(2,1)S(1)} custom-call(s32[4]{0:T(128)S(1)} %multiply_add_fusion.1.order_ref, bf16[1024,512]{1,0:T(8,128)(2,1)S(1)} %copy-done.26, bf16[1024,512]{1,0:T(8,128)(2,1)S(1)} %teacher_attention.3.b_ref, bf16[1024,4096]{1,0:T(8,128)(2,1)} %p_ref.5), custom_call_target="tpu_custom_call" | custom-call | flops 4000000000 | tf_op jit(solution)/shard_map/project/pallas_call | solution.py:76
  149.1 2.0 add_convert_fusion
  151.4 4.5 %reduce-scatter.5.cloned.1.call-done.refs_4_ = bf16[2,1024,256]{2,1,0:T(8,128)(2,1)} async-done(((bf16[8,1024,256]{2,1,0:T(8,128)(2,1)}), bf16[2,1024,256]{2,1,0:T(8,128)(2,1)}) %reduce-scatter.5.cloned.1.call-update) | async-done | bytes 1048592 | tf_op jit(solution)/shard_map/reduce_scatter | solution.py:406
  157.0 2.8 collective-permute-start.10
  162.6 12.4 %student_project.1.refs_1_.refs_2_.refs_3_ = bf16[1024,768]{1,0:T(8,128)(2,1)} custom-call(s32[10]{0:T(128)S(1)} %stack.115.refs_0_, bf16[128,4096]{1,0:T(8,128)(2,1)S(1)} %bitcast.38, bf16[128,4096]{1,0:T(8,128)(2,1)S(1)} %collective-permute-done.refs_2_.refs_4_.refs_5_, bf16[128,4096]{1,0:T(8,128)(2,1)S(1)} %collective-permute-done.2.refs_3_.refs_5_.refs_6_, ...), custom_call_target="tpu_custom_call" | custom-call | flops 8999999488 | tf_op jit(solution)/shard_map/student_project/pallas_call | solution.py:131
  176.4 10.8 %student_attention.2 = (bf16[1024,256]{1,0:T(8,128)(2,1)S(1)}, f32[1024,256]{1,0:T(8,128)S(1)}) custom-call(s32[1]{0:T(128)} %bitcast.22.refs_0_, bf16[1024,768]{1,0:T(8,128)(2,1)S(1)} %copy-done.30, bf16[1024,768]{1,0:T(8,128)(2,1)S(1)} %copy-done.30, bf16[1024,768]{1,0:T(8,128)(2,1)S(1)} %copy-done.30, bf16[2,1024,256]{2,1,0:T(8,128)(2,1)S(1)} %copy-done.1, ...), custom_call_target="tpu_custom_call" | custom-call | flops 11000000512 | tf_op jit(solution)/shard_map/student_attention/pallas_call | solution.py:281
  188.2 7.5 %weight_grad.5 = bf16[8,256,256]{2,1,0:T(8,128)(2,1)} custom-call(s32[10]{0:T(128)S(1)} %stack.115.refs_0_, s32[8]{0:T(128)S(1)} %stack.133.refs_1_, bf16[1024,256]{1,0:T(8,128)(2,1)S(1)} %get-tuple-element.50.refs_2_, bf16[128,4096]{1,0:T(8,128)(2,1)S(1)} %bitcast.39, bf16[128,4096]{1,0:T(8,128)(2,1)S(1)} %collective-permute-done.refs_2_.refs_4_.refs_5_, ...), custom_call_target="tpu_custom_call" | custom-call | flops 4000000000 | tf_op jit(solution)/shard_map/weight_grad/pallas_call | solution.py:175
  199.0 6.8 %weight_grad.4.a_ref = bf16[8,256,256]{2,1,0:T(8,128)(2,1)S(1)} custom-call(s32[10]{0:T(128)S(1)} %stack.115.refs_0_, s32[8]{0:T(128)S(1)} %stack.124.refs_1_, bf16[1024,256]{1,0:T(8,128)(2,1)S(1)} %copy-done.29, bf16[128,4096]{1,0:T(8,128)(2,1)S(1)} %bitcast.40, bf16[128,4096]{1,0:T(8,128)(2,1)S(1)} %collective-permute-done.refs_2_.refs_4_.refs_5_, ...), custom_call_target="tpu_custom_call" | custom-call | flops 4000000000 | tf_op jit(solution)/shard_map/weight_grad/pallas_call | solution.py:175
  213.7 2.9 collective-permute-start.13
  221.5 7.8 %collective-permute-done.13.refs_2_ = bf16[256,256]{1,0:T(8,128)(2,1)S(1)} collective-permute-done((bf16[256,256]{1,0:T(8,128)(2,1)}, bf16[256,256]{1,0:T(8,128)(2,1)S(1)}, u32[]{:S(2)}, u32[]{:S(2)}) %collective-permute-start.13) | collective-permute-done | bytes 131104 | tf_op jit(solution)/shard_map/ppermute | solution.py:347
  231.7 10.8 %student_attention.3 = (bf16[1024,256]{1,0:T(8,128)(2,1)S(1)}, bf16[1024,256]{1,0:T(8,128)(2,1)S(1)}) custom-call(s32[1]{0:T(128)} %constant.217.clone.1.refs_0_, bf16[1024,768]{1,0:T(8,128)(2,1)S(1)} %copy-done.31, bf16[1024,768]{1,0:T(8,128)(2,1)S(1)} %copy-done.31, bf16[1024,768]{1,0:T(8,128)(2,1)S(1)} %copy-done.31, ...), custom_call_target="tpu_custom_call" | custom-call | flops 11000000512 | tf_op jit(solution)/shard_map/student_attention/pallas_call | solution.py:281
  242.6 8.3 %weight_grad.7 = bf16[8,512,256]{2,1,0:T(8,128)(2,1)} custom-call(s32[10]{0:T(128)S(1)} %stack.115.refs_0_, s32[8]{0:T(128)S(1)} %stack.133.refs_1_, bf16[1024,256]{1,0:T(8,128)(2,1)S(1)} %get-tuple-element.71.refs_2_, bf16[1024,256]{1,0:T(8,128)(2,1)S(1)} %get-tuple-element.72.refs_3_, bf16[128,4096]{1,0:T(8,128)(2,1)S(1)} %bitcast.41, ...), custom_call_target="tpu_custom_call" | custom-call | flops 4000000000 | tf_op jit(solution)/shard_map/weight_grad/pallas_call | solution.py:175
  250.9 8.3 %weight_grad.6.a_ref = bf16[8,512,256]{2,1,0:T(8,128)(2,1)} custom-call(s32[10]{0:T(128)S(1)} %stack.115.refs_0_, s32[8]{0:T(128)S(1)} %stack.124.refs_1_, bf16[1024,256]{1,0:T(8,128)(2,1)S(1)} %get-tuple-element.71.refs_2_, bf16[1024,256]{1,0:T(8,128)(2,1)S(1)} %get-tuple-element.72.refs_3_, bf16[128,4096]{1,0:T(8,128)(2,1)S(1)} %bitcast.42, ...), custom_call_target="tpu_custom_call" | custom-call | flops 4000000000 | tf_op jit(solution)/shard_map/weight_grad/pallas_call | solution.py:175
  262.1 2.1 pair_sum.3
  264.2 2.9 collective-permute-start.20
  267.1 2.8 collective-permute-start.22
  270.6 14.9 %collective-permute-done.20.refs_9_ = bf16[512,256]{1,0:T(8,128)(2,1)S(1)} collective-permute-done((bf16[512,256]{1,0:T(8,128)(2,1)S(1)}, bf16[512,256]{1,0:T(8,128)(2,1)S(1)}, u32[]{:S(2)}, u32[]{:S(2)}) %collective-permute-start.20) | collective-permute-done | bytes 262176 | tf_op jit(solution)/shard_map/ppermute | solution.py:347
  285.8 11.2 %collective-permute-done.25.refs_14_ = bf16[512,256]{1,0:T(8,128)(2,1)S(1)} collective-permute-done((bf16[512,256]{1,0:T(8,128)(2,1)S(1)}, bf16[512,256]{1,0:T(8,128)(2,1)S(1)}, u32[]{:S(2)}, u32[]{:S(2)}) %collective-permute-start.25) | collective-permute-done | bytes 262176 | tf_op jit(solution)/shard_map/ppermute | solution.py:347
  (141 shorter events, 47.0 us)
Async XLA Ops:
  7.2 62.8 %all-gather.2.cloned.1.call-start = ((), (), s32[]{:S(2)}) async-start(), calls=%async_computation.2 | async-start | bytes 6684672 | tf_op jit(solution)/shard_map/all_gather | solution.py:392
  9.1 146.9 %reduce-scatter.5.cloned.1.call-start = ((), (), s32[]{:S(2)}) async-start(), calls=%async_computation.4 | async-start | bytes 5242880 | tf_op jit(solution)/shard_map/reduce_scatter | solution.py:406
  9.1 26.3 %collective-permute-start = (bf16[128,4096]{1,0:T(8,128)(2,1)}, bf16[128,4096]{1,0:T(8,128)(2,1)S(1)}, u32[]{:S(2)}, u32[]{:S(2)}) collective-permute-start(bf16[128,4096]{1,0:T(8,128)(2,1)} %bitcast.35), channel_id=1, source_target_pairs={{0,2},{2,4},{4,6},{6,0},{1,3},{3,5},{5,7},{7,1},{8,10},{10,12},{12... | collective-permute-start | bytes 3145736 | tf_op jit(solution)/shard_map/ppermute | solution.py:312
  10.8 25.2 %collective-permute-start.2 = (bf16[128,4096]{1,0:T(8,128)(2,1)}, bf16[128,4096]{1,0:T(8,128)(2,1)S(1)}, u32[]{:S(2)}, u32[]{:S(2)}) collective-permute-start(bf16[128,4096]{1,0:T(8,128)(2,1)} %bitcast.36), channel_id=1, source_target_pairs={{0,6},{2,0},{4,2},{6,4},{1,7},{3,1},{5,3},{7,5},{8,14},{10,8},{12,... | collective-permute-start | bytes 3145736 | tf_op jit(solution)/shard_map/ppermute | solution.py:312
  12.4 43.8 %collective-permute-start.4 = (bf16[128,4096]{1,0:T(8,128)(2,1)}, bf16[128,4096]{1,0:T(8,128)(2,1)S(1)}, u32[]{:S(2)}, u32[]{:S(2)}) collective-permute-start(bf16[128,4096]{1,0:T(8,128)(2,1)} %bitcast.37), channel_id=1, source_target_pairs={{0,1},{1,0},{2,3},{3,2},{4,5},{5,4},{6,7},{7,6},{8,9},{9,8},{10,11... | collective-permute-start | bytes 3145736 | tf_op jit(solution)/shard_map/ppermute | solution.py:312
  35.4 20.8 %collective-permute-start.1 = (bf16[64,4096]{1,0:T(8,128)(2,1)S(1)}, bf16[64,4096]{1,0:T(8,128)(2,1)S(1)}, u32[]{:S(2)}, u32[]{:S(2)}) collective-permute-start(bf16[64,4096]{1,0:T(8,128)(2,1)S(1)} %slice.16), channel_id=1, source_target_pairs={{0,2},{2,4},{4,6},{6,0},{1,3},{3,5},{5,7},{7,1},{8,10},{10,12},{12... | collective-permute-start | bytes 1572872 | tf_op jit(solution)/shard_map/ppermute | solution.py:312
  36.0 124.5 %copy-start = (bf16[128,4096]{1,0:T(8,128)(2,1)}, bf16[128,4096]{1,0:T(8,128)(2,1)S(1)}, u32[]{:S(2)}) copy-start(bf16[128,4096]{1,0:T(8,128)(2,1)S(1)} %collective-permute-done.2.refs_3_.refs_5_.refs_6_) | copy-start | bytes 3145732
  36.0 21.9 %collective-permute-start.3 = (bf16[64,4096]{1,0:T(8,128)(2,1)S(1)}, bf16[64,4096]{1,0:T(8,128)(2,1)S(1)}, u32[]{:S(2)}, u32[]{:S(2)}) collective-permute-start(bf16[64,4096]{1,0:T(8,128)(2,1)S(1)} %slice.17), channel_id=1, source_target_pairs={{0,6},{2,0},{4,2},{6,4},{1,7},{3,1},{5,3},{7,5},{8,14},{10,8},{12,... | collective-permute-start | bytes 1572872 | tf_op jit(solution)/shard_map/ppermute | solution.py:312
  81.2 135.3 %reduce-scatter.3.cloned.1.call-start = ((), (), s32[]{:S(2)}) async-start(), calls=%async_computation.3 | async-start | bytes 2621440 | tf_op jit(solution)/shard_map/reduce_scatter | solution.py:421
  87.5 56.5 %copy-start.26 = (bf16[1024,512]{1,0:T(8,128)(2,1)S(1)}, bf16[1024,512]{1,0:T(8,128)(2,1)}, u32[]{:S(2)}) copy-start(bf16[1024,512]{1,0:T(8,128)(2,1)} %copy-done.23) | copy-start | bytes 3145732
  87.6 61.5 %collective-permute-start.7 = (bf16[4,1024,256]{2,1,0:T(8,128)(2,1)S(1)}, bf16[4,1024,256]{2,1,0:T(8,128)(2,1)S(1)}, u32[]{:S(2)}, u32[]{:S(2)}) collective-permute-start(bf16[4,1024,256]{2,1,0:T(8,128)(2,1)S(1)} %project.4), channel_id=1, source_target_pairs={{0,1},{1,0},{2,3},{3,2},{4,5},{5,4},{6,7},{7,6},{8,9},{9,8},{10,11... | collective-permute-start | bytes 6291464 | tf_op jit(solution)/shard_map/ppermute | solution.py:312
  89.8 49.1 %collective-permute-start.5 = (bf16[128,4096]{1,0:T(8,128)(2,1)S(1)}, bf16[128,4096]{1,0:T(8,128)(2,1)S(1)}, u32[]{:S(2)}, u32[]{:S(2)}) collective-permute-start(bf16[128,4096]{1,0:T(8,128)(2,1)S(1)} %copy-done.40), channel_id=1, source_target_pairs={{0,2},{2,4},{4,6},{6,0},{1,3},{3,5},{5,7},{7,1},{8,10},{10,12},{12... | collective-permute-start | bytes 3145736 | tf_op jit(solution)/shard_map/ppermute | solution.py:312
  90.4 48.5 %collective-permute-start.6 = (bf16[128,4096]{1,0:T(8,128)(2,1)S(1)}, bf16[128,4096]{1,0:T(8,128)(2,1)S(1)}, u32[]{:S(2)}, u32[]{:S(2)}) collective-permute-start(bf16[128,4096]{1,0:T(8,128)(2,1)S(1)} %copy-done.40), channel_id=1, source_target_pairs={{0,6},{2,0},{4,2},{6,4},{1,7},{3,1},{5,3},{7,5},{8,14},{10,8},{12,... | collective-permute-start | bytes 3145736 | tf_op jit(solution)/shard_map/ppermute | solution.py:312
  139.8 20.7 %collective-permute-start.8 = (bf16[64,4096]{1,0:T(8,128)(2,1)}, bf16[64,4096]{1,0:T(8,128)(2,1)}, u32[]{:S(2)}, u32[]{:S(2)}) collective-permute-start(bf16[64,4096]{1,0:T(8,128)(2,1)} %slice.14), channel_id=1, source_target_pairs={{0,2},{2,4},{4,6},{6,0},{1,3},{3,5},{5,7},{7,1},{8,10},{10,12},{12... | collective-permute-start | bytes 1572872 | tf_op jit(solution)/shard_map/ppermute | solution.py:312
  141.5 18.9 %collective-permute-start.9 = (bf16[64,4096]{1,0:T(8,128)(2,1)}, bf16[64,4096]{1,0:T(8,128)(2,1)}, u32[]{:S(2)}, u32[]{:S(2)}) collective-permute-start(bf16[64,4096]{1,0:T(8,128)(2,1)} %slice.15), channel_id=1, source_target_pairs={{0,6},{2,0},{4,2},{6,4},{1,7},{3,1},{5,3},{7,5},{8,14},{10,8},{12,... | collective-permute-start | bytes 1572872 | tf_op jit(solution)/shard_map/ppermute | solution.py:312
  157.0 17.9 %collective-permute-start.10 = (bf16[1024,256]{1,0:T(8,128)(2,1)S(1)}, bf16[1024,256]{1,0:T(8,128)(2,1)S(1)}, u32[]{:S(2)}, u32[]{:S(2)}) collective-permute-start(bf16[1024,256]{1,0:T(8,128)(2,1)S(1)} %dynamic-slice_bitcast_fusion), channel_id=1, source_target_pairs={{0,1},{1,0},{2,3},{3,2},{4,5},{5,4},{6,7},{7,6},{8,9},{9,8},{10,11... | collective-permute-start | bytes 1572872 | tf_op jit(solution)/shard_map/ppermute | solution.py:312
  195.7 10.1 %collective-permute-start.11 = (bf16[8,256,256]{2,1,0:T(8,128)(2,1)}, bf16[8,256,256]{2,1,0:T(8,128)(2,1)S(1)}, u32[]{:S(2)}, u32[]{:S(2)}) collective-permute-start(bf16[8,256,256]{2,1,0:T(8,128)(2,1)} %weight_grad.5), channel_id=1, source_target_pairs={{0,8},{8,0},{1,9},{9,1},{2,10},{10,2},{3,11},{11,3},{4,12},{12,4},... | collective-permute-start | bytes 3145736 | tf_op jit(solution)/shard_map/ppermute | solution.py:312
  212.1 7.9 %collective-permute-start.12 = (bf16[256,256]{1,0:T(8,128)(2,1)}, bf16[256,256]{1,0:T(8,128)(2,1)S(1)}, u32[]{:S(2)}, u32[]{:S(2)}) collective-permute-start(bf16[256,256]{1,0:T(8,128)(2,1)} %get-tuple-element.53), channel_id=1, source_target_pairs={{0,16},{16,32},{32,48},{48,0},{64,80},{80,96},{96,112},{112,64},{1... | collective-permute-start | bytes 393224 | tf_op jit(solution)/shard_map/ppermute | solution.py:347
  213.7 15.6 %collective-permute-start.13 = (bf16[256,256]{1,0:T(8,128)(2,1)}, bf16[256,256]{1,0:T(8,128)(2,1)S(1)}, u32[]{:S(2)}, u32[]{:S(2)}) collective-permute-start(bf16[256,256]{1,0:T(8,128)(2,1)} %get-tuple-element.54), channel_id=1, source_target_pairs={{0,32},{16,48},{32,0},{48,16},{64,96},{80,112},{96,64},{112,80},{1... | collective-permute-start | bytes 393224 | tf_op jit(solution)/shard_map/ppermute | solution.py:347
  216.6 25.9 %collective-permute-start.14 = (bf16[256,256]{1,0:T(8,128)(2,1)}, bf16[256,256]{1,0:T(8,128)(2,1)S(1)}, u32[]{:S(2)}, u32[]{:S(2)}) collective-permute-start(bf16[256,256]{1,0:T(8,128)(2,1)} %copy-done.22), channel_id=1, source_target_pairs={{0,48},{16,0},{32,16},{48,32},{64,112},{80,64},{96,80},{112,96},{1... | collective-permute-start | bytes 393224 | tf_op jit(solution)/shard_map/ppermute | solution.py:347
  217.9 24.6 %collective-permute-start.15 = (bf16[256,256]{1,0:T(8,128)(2,1)}, bf16[256,256]{1,0:T(8,128)(2,1)S(1)}, u32[]{:S(2)}, u32[]{:S(2)}) collective-permute-start(bf16[256,256]{1,0:T(8,128)(2,1)} %copy-done.21), channel_id=1, source_target_pairs={{0,64},{16,80},{32,96},{48,112},{64,0},{80,16},{96,32},{112,48},{1... | collective-permute-start | bytes 393224 | tf_op jit(solution)/shard_map/ppermute | solution.py:347
  218.6 23.9 %collective-permute-start.16 = (bf16[256,256]{1,0:T(8,128)(2,1)}, bf16[256,256]{1,0:T(8,128)(2,1)S(1)}, u32[]{:S(2)}, u32[]{:S(2)}) collective-permute-start(bf16[256,256]{1,0:T(8,128)(2,1)} %copy-done.20), channel_id=1, source_target_pairs={{0,80},{16,96},{32,112},{48,64},{64,16},{80,32},{96,48},{112,0},{1... | collective-permute-start | bytes 393224 | tf_op jit(solution)/shard_map/ppermute | solution.py:347
  220.1 22.5 %collective-permute-start.17 = (bf16[256,256]{1,0:T(8,128)(2,1)}, bf16[256,256]{1,0:T(8,128)(2,1)S(1)}, u32[]{:S(2)}, u32[]{:S(2)}) collective-permute-start(bf16[256,256]{1,0:T(8,128)(2,1)} %copy-done.19), channel_id=1, source_target_pairs={{0,96},{16,112},{32,64},{48,80},{64,32},{80,48},{96,0},{112,16},{1... | collective-permute-start | bytes 393224 | tf_op jit(solution)/shard_map/ppermute | solution.py:347
  229.2 13.3 %collective-permute-start.18 = (bf16[256,256]{1,0:T(8,128)(2,1)S(1)}, bf16[256,256]{1,0:T(8,128)(2,1)S(1)}, u32[]{:S(2)}, u32[]{:S(2)}) collective-permute-start(bf16[256,256]{1,0:T(8,128)(2,1)S(1)} %get-tuple-element.59), channel_id=1, source_target_pairs={{0,112},{16,64},{32,80},{48,96},{64,48},{80,0},{96,16},{112,32},{1... | collective-permute-start | bytes 393224 | tf_op jit(solution)/shard_map/ppermute | solution.py:347
  250.9 8.3 %collective-permute-start.19 = (bf16[8,512,256]{2,1,0:T(8,128)(2,1)}, bf16[8,512,256]{2,1,0:T(8,128)(2,1)S(1)}, u32[]{:S(2)}, u32[]{:S(2)}) collective-permute-start(bf16[8,512,256]{2,1,0:T(8,128)(2,1)} %weight_grad.7), channel_id=1, source_target_pairs={{0,8},{8,0},{1,9},{9,1},{2,10},{10,2},{3,11},{11,3},{4,12},{12,4},... | collective-permute-start | bytes 6291464 | tf_op jit(solution)/shard_map/ppermute | solution.py:312
  264.2 21.2 %collective-permute-start.20 = (bf16[512,256]{1,0:T(8,128)(2,1)S(1)}, bf16[512,256]{1,0:T(8,128)(2,1)S(1)}, u32[]{:S(2)}, u32[]{:S(2)}) collective-permute-start(bf16[512,256]{1,0:T(8,128)(2,1)S(1)} %get-tuple-element.74), channel_id=1, source_target_pairs={{0,16},{16,32},{32,48},{48,0},{64,80},{80,96},{96,112},{112,64},{1... | collective-permute-start | bytes 786440 | tf_op jit(solution)/shard_map/ppermute | solution.py:347
  267.1 18.4 %collective-permute-start.21 = (bf16[512,256]{1,0:T(8,128)(2,1)S(1)}, bf16[512,256]{1,0:T(8,128)(2,1)S(1)}, u32[]{:S(2)}, u32[]{:S(2)}) collective-permute-start(bf16[512,256]{1,0:T(8,128)(2,1)S(1)} %get-tuple-element.75), channel_id=1, source_target_pairs={{0,32},{16,48},{32,0},{48,16},{64,96},{80,112},{96,64},{112,80},{1... | collective-permute-start | bytes 786440 | tf_op jit(solution)/shard_map/ppermute | solution.py:347
  267.1 18.7 %collective-permute-start.22 = (bf16[512,256]{1,0:T(8,128)(2,1)S(1)}, bf16[512,256]{1,0:T(8,128)(2,1)S(1)}, u32[]{:S(2)}, u32[]{:S(2)}) collective-permute-start(bf16[512,256]{1,0:T(8,128)(2,1)S(1)} %get-tuple-element.76), channel_id=1, source_target_pairs={{0,48},{16,0},{32,16},{48,32},{64,112},{80,64},{96,80},{112,96},{1... | collective-permute-start | bytes 786440 | tf_op jit(solution)/shard_map/ppermute | solution.py:347
  269.9 16.0 %collective-permute-start.23 = (bf16[512,256]{1,0:T(8,128)(2,1)S(1)}, bf16[512,256]{1,0:T(8,128)(2,1)S(1)}, u32[]{:S(2)}, u32[]{:S(2)}) collective-permute-start(bf16[512,256]{1,0:T(8,128)(2,1)S(1)} %get-tuple-element.77), channel_id=1, source_target_pairs={{0,64},{16,80},{32,96},{48,112},{64,0},{80,16},{96,32},{112,48},{1... | collective-permute-start | bytes 786440 | tf_op jit(solution)/shard_map/ppermute | solution.py:347
  270.6 15.3 %collective-permute-start.24 = (bf16[512,256]{1,0:T(8,128)(2,1)S(1)}, bf16[512,256]{1,0:T(8,128)(2,1)S(1)}, u32[]{:S(2)}, u32[]{:S(2)}) collective-permute-start(bf16[512,256]{1,0:T(8,128)(2,1)S(1)} %get-tuple-element.78), channel_id=1, source_target_pairs={{0,80},{16,96},{32,112},{48,64},{64,16},{80,32},{96,48},{112,0},{1... | collective-permute-start | bytes 786440 | tf_op jit(solution)/shard_map/ppermute | solution.py:347
  285.5 11.6 %collective-permute-start.25 = (bf16[512,256]{1,0:T(8,128)(2,1)S(1)}, bf16[512,256]{1,0:T(8,128)(2,1)S(1)}, u32[]{:S(2)}, u32[]{:S(2)}) collective-permute-start(bf16[512,256]{1,0:T(8,128)(2,1)S(1)} %get-tuple-element.79), channel_id=1, source_target_pairs={{0,96},{16,112},{32,64},{48,80},{64,32},{80,48},{96,0},{112,16},{1... | collective-permute-start | bytes 786440 | tf_op jit(solution)/shard_map/ppermute | solution.py:347
  285.5 11.6 %collective-permute-start.26 = (bf16[512,256]{1,0:T(8,128)(2,1)S(1)}, bf16[512,256]{1,0:T(8,128)(2,1)S(1)}, u32[]{:S(2)}, u32[]{:S(2)}) collective-permute-start(bf16[512,256]{1,0:T(8,128)(2,1)S(1)} %get-tuple-element.80), channel_id=1, source_target_pairs={{0,112},{16,64},{32,80},{48,96},{64,48},{80,0},{96,16},{112,32},{1... | collective-permute-start | bytes 786440 | tf_op jit(solution)/shard_map/ppermute | solution.py:347
  (39 other events, 192.0 us)
Sparse Core Ops, SparseCore 0:
  9.7 60.2 all-gather.1
  81.3 74.5 reduce-scatter.4
  158.5 29.2 reduce-scatter.2

commit v3 on v2

v3 whole, which is shorter than its diff:
```python
import functools

import jax
import jax.numpy as jnp
from jax import lax
from jax.experimental import pallas as pl
from jax.experimental.pallas import tpu as pltpu
from jax.sharding import Mesh, PartitionSpec as P

HEAD = 128
FACTOR = HEAD ** (-0.5)
LOG2E = 1.4426950408889634
BLOCK = 256
SEQ = 1024
DP = ("ylo", "z", "core")
TENSOR = ("x", "yhi")
NT = (((1,), (1,)), ((), ()))
VMEM = pltpu.CompilerParams(vmem_limit_bytes=60 * 1024 * 1024)


def cost(us, moved=0):
    return pl.CostEstimate(flops=int(us * 1.0e9), bytes_accessed=moved, transcendentals=0)


def dot(a, b):
    return jnp.dot(a, b, preferred_element_type=jnp.float32)


def parts_of(number):
    first = number * BLOCK
    own = (first, first + BLOCK)
    return [(0, first), own] if first else [own]


def teacher_kernel(q_ref, k_ref, v_ref, o_ref):
    row = lax.broadcasted_iota(jnp.int32, (BLOCK, BLOCK), 0)
    col = lax.broadcasted_iota(jnp.int32, (BLOCK, BLOCK), 1)
    for number in range(SEQ // BLOCK):
        first = number * BLOCK
        limit = first + BLOCK
        parts = parts_of(number)
        for head in range(2):
            cols = slice(head * HEAD, head * HEAD + HEAD)
            queries = q_ref[first:limit, cols]
            scores = [
                lax.dot_general(queries, k_ref[lo:hi, :], NT, preferred_element_type=jnp.float32)
                for lo, hi in parts
            ]
            scores[-1] = jnp.where(col <= row, scores[-1], -1e30)
            top = functools.reduce(
                jnp.maximum, [jnp.max(s, axis=1, keepdims=True) for s in scores]
            )
            weights = [jnp.exp2((s - top) * (FACTOR * LOG2E)) for s in scores]
            total = sum(jnp.sum(w, axis=1, keepdims=True) for w in weights)
            context = sum(
                dot(w.astype(jnp.bfloat16), v_ref[lo:hi, :]) for w, (lo, hi) in zip(weights, parts)
            )
            o_ref[first:limit, cols] = (context / total).astype(jnp.bfloat16)


def teacher_attention(queries, keys, values, half, before=()):
    steps = queries.shape[1] // (4 * HEAD)
    pair = pl.BlockSpec((SEQ, 2 * HEAD), lambda h: (0, half * steps + h))
    one = pl.BlockSpec((SEQ, HEAD), lambda h: (0, 0))
    return pl.pallas_call(
        lambda q_ref, k_ref, v_ref, *rest: teacher_kernel(q_ref, k_ref, v_ref, rest[-1]),
        grid=(steps,),
        in_specs=[pair, one, one] + [pl.BlockSpec(memory_space=pl.ANY)] * len(before),
        out_specs=pair,
        out_shape=jax.ShapeDtypeStruct(queries.shape, jnp.bfloat16),
        input_output_aliases={3: 0} if before else {},
        compiler_params=VMEM,
        cost_estimate=cost(1 if before else 40),
        name="teacher_attention",
    )(queries, keys, values, *before)


def project_kernel(order_ref, context_ref, p_ref, o_ref):
    o_ref[0] = dot(context_ref[...], p_ref[...]).astype(jnp.bfloat16)


def project(order, context, projector, weight):
    rows = projector.shape[0]
    count = order.shape[0]
    return pl.pallas_call(
        project_kernel,
        grid_spec=pltpu.PrefetchScalarGridSpec(
            num_scalar_prefetch=1,
            grid=(count,),
            in_specs=[
                pl.BlockSpec(context.shape, lambda g, order: (0, 0)),
                pl.BlockSpec((rows, 256), lambda g, order: (0, order[g])),
            ],
            out_specs=pl.BlockSpec((1, SEQ, 256), lambda g, order: (g, 0, 0)),
        ),
        out_shape=jax.ShapeDtypeStruct((count, SEQ, 256), jnp.bfloat16),
        compiler_params=VMEM,
        cost_estimate=cost(weight),
        name="project",
    )(order, context, projector)


def student_project_kernel(count, *refs):
    at_ref, pieces, near_ref, far_ref = refs[0], refs[2 : 2 + count], refs[2 + count], refs[3 + count]
    o_ref, rows_ref, total = refs[-3:]
    step = pl.program_id(0)
    for number, ref in enumerate(pieces):
        rows_ref[pl.ds(pl.multiple_of(at_ref[number], 64), ref.shape[0]), :] = ref[...]

    @pl.when(step == 0)
    def _():
        total[...] = dot(rows_ref[...], near_ref[...])

    @pl.when(step == 1)
    def _():
        total[...] += dot(rows_ref[...], near_ref[...])

    @pl.when(step == 2)
    def _():
        total[...] += dot(rows_ref[...], far_ref[...])

    @pl.when(step == 3)
    def _():
        o_ref[...] = (total[...] + dot(rows_ref[...], far_ref[...])).astype(jnp.bfloat16)


def student_project(places, order, pieces, near, far, before=()):
    depth, cols = near.shape
    half = SEQ // 2
    block = 1024
    side = 1 if before else 0
    count = len(pieces)
    return pl.pallas_call(
        lambda *refs: student_project_kernel(count, *refs),
        grid_spec=pltpu.PrefetchScalarGridSpec(
            num_scalar_prefetch=2,
            grid=(4,),
            in_specs=[
                pl.BlockSpec((p.shape[0], block), lambda k, at, order: (0, order[k]))
                for p in pieces
            ]
            + [
                pl.BlockSpec((block, cols), lambda k, at, order: (jnp.minimum(k, 1), 0)),
                pl.BlockSpec((block, cols), lambda k, at, order: (jnp.maximum(k - 2, 0), 0)),
            ]
            + [pl.BlockSpec(memory_space=pl.ANY)] * len(before),
            out_specs=[
                pl.BlockSpec((half, cols), lambda k, at, order: (side, 0)),
                pl.BlockSpec((half, block), lambda k, at, order: (side, order[k])),
            ],
            scratch_shapes=[pltpu.VMEM((half, cols), jnp.float32)],
        ),
        out_shape=[
            jax.ShapeDtypeStruct((SEQ, cols), jnp.bfloat16),
            jax.ShapeDtypeStruct((SEQ, 2 * depth), jnp.bfloat16),
        ],
        input_output_aliases={4 + count: 0, 5 + count: 1} if before else {},
        compiler_params=VMEM,
        cost_estimate=cost(9),
        name="student_project",
    )(places, order, *pieces, near, far, *before)


def weight_grad_ring_kernel(order_ref, grad_ref, rows_ref, o_ref):
    product = dot(grad_ref[...], rows_ref[...]).astype(jnp.bfloat16)
    o_ref[0, 0, 0] = product[:, :256]
    o_ref[0, 1, 0] = product[:, 256:]


def weight_grad_ring(grads, rows):
    cols = grads.shape[0]
    order = jnp.array([k % 2 * 4 + k // 2 for k in range(8)], jnp.int32)
    return pl.pallas_call(
        weight_grad_ring_kernel,
        grid_spec=pltpu.PrefetchScalarGridSpec(
            num_scalar_prefetch=1,
            grid=(8,),
            in_specs=[
                pl.BlockSpec(grads.shape, lambda k, order: (0, 0)),
                pl.BlockSpec((SEQ, 512), lambda k, order: (0, order[k])),
            ],
            out_specs=pl.BlockSpec(
                (1, 2, 1, cols, 256), lambda k, order: (k // 2, 0, k % 2, 0, 0)
            ),
        ),
        out_shape=jax.ShapeDtypeStruct((4, 2, 2, cols, 256), jnp.bfloat16),
        compiler_params=VMEM,
        cost_estimate=cost(4),
        name="weight_grad_ring",
    )(order, grads, rows)


def weight_grad_kernel(core_ref, order_ref, grad_ref, rows_ref, kept_ref, sent_ref):
    product = dot(grad_ref[...], rows_ref[...]).astype(jnp.bfloat16)

    @pl.when(core_ref[0] == 0)
    def _():
        kept_ref[0] = product[:, :256]
        sent_ref[0] = product[:, 256:]

    @pl.when(core_ref[0] == 1)
    def _():
        kept_ref[0] = product[:, 256:]
        sent_ref[0] = product[:, :256]


def weight_grad(core, order, grads, rows):
    cols = grads.shape[0]
    out = pl.BlockSpec((1, cols, 256), lambda k, core, order: (k, 0, 0))
    return pl.pallas_call(
        weight_grad_kernel,
        grid_spec=pltpu.PrefetchScalarGridSpec(
            num_scalar_prefetch=2,
            grid=(8,),
            in_specs=[
                pl.BlockSpec(grads.shape, lambda k, core, order: (0, 0)),
                pl.BlockSpec((SEQ, 512), lambda k, core, order: (0, order[k])),
            ],
            out_specs=[out, out],
        ),
        out_shape=[jax.ShapeDtypeStruct((8, cols, 256), jnp.bfloat16)] * 2,
        compiler_params=VMEM,
        cost_estimate=cost(4),
        name="weight_grad",
    )(core, order, grads, rows)


def pair_kernel(a_ref, b_ref, *outs):
    for number, ref in enumerate(outs):
        ref[...] = (
            a_ref[number].astype(jnp.float32) + b_ref[number].astype(jnp.float32)
        ).astype(jnp.bfloat16)


def pair_sum(a, b):
    return pl.pallas_call(
        pair_kernel,
        out_shape=[jax.ShapeDtypeStruct(a.shape[1:], jnp.bfloat16) for _ in range(a.shape[0])],
        compiler_params=VMEM,
        cost_estimate=cost(3),
        name="pair_sum",
    )(a, b)


def forward_kernel(y_ref, q_in, k_in, v_in, q_ref, kv_ref, probs_ref, context_ref, vt):
    y = y_ref[0]
    for block in range(4):
        for which, side in ((0, y), (1, 1 - y)):
            rows = slice((4 * which + block) * HEAD, (4 * which + block) * HEAD + HEAD)
            at = pl.ds(pl.multiple_of((2 * block + side) * HEAD, HEAD), HEAD)
            q_ref[at, :] = q_in[rows, :]
            kv_ref[at, :HEAD] = k_in[rows, :]
            kv_ref[at, HEAD:] = v_in[rows, :]
    vt[...] = kv_ref[:, HEAD:].T
    key = lax.broadcasted_iota(jnp.int32, (BLOCK, BLOCK), 0)
    query = lax.broadcasted_iota(jnp.int32, (BLOCK, BLOCK), 1)
    for number in range(SEQ // BLOCK):
        first = number * BLOCK
        limit = first + BLOCK
        parts = parts_of(number)
        for head in range(2):
            cols = slice(head * HEAD, head * HEAD + HEAD)
            queries = q_ref[first:limit, cols]
            scores = [
                lax.dot_general(
                    kv_ref[lo:hi, :HEAD], queries, NT, preferred_element_type=jnp.float32
                )
                for lo, hi in parts
            ]
            scores[-1] = jnp.where(key <= query, scores[-1], -1e30)
            top = functools.reduce(
                jnp.maximum, [jnp.max(s, axis=0, keepdims=True) for s in scores]
            )
            weights = [jnp.exp2((s - top) * (FACTOR * LOG2E)) for s in scores]
            scale = 1.0 / sum(jnp.sum(w, axis=0, keepdims=True) for w in weights)
            context = 0.0
            for w, (lo, hi) in zip(weights, parts):
                rounded = (w * scale).astype(jnp.bfloat16)
                probs_ref[head, lo:hi, first:limit] = rounded
                context += dot(vt[:, lo:hi], rounded)
            context_ref[first:limit, cols] = context.T


def student_forward(y, projected):
    pair = pl.BlockSpec((SEQ, 2 * HEAD), lambda i, y: (0, i))
    both = pl.BlockSpec((SEQ, 2 * HEAD), lambda i, y: (0, 0))
    return pl.pallas_call(
        forward_kernel,
        grid_spec=pltpu.PrefetchScalarGridSpec(
            num_scalar_prefetch=1,
            grid=(2,),
            in_specs=[
                pair,
                pl.BlockSpec((SEQ, HEAD), lambda i, y: (0, 4)),
                pl.BlockSpec((SEQ, HEAD), lambda i, y: (0, 5)),
            ],
            out_specs=[pair, both, pl.BlockSpec((2, SEQ, SEQ), lambda i, y: (i, 0, 0)), pair],
            scratch_shapes=[pltpu.VMEM((HEAD, SEQ), jnp.bfloat16)],
        ),
        out_shape=[
            jax.ShapeDtypeStruct((SEQ, 4 * HEAD), jnp.bfloat16),
            jax.ShapeDtypeStruct((SEQ, 2 * HEAD), jnp.bfloat16),
            jax.ShapeDtypeStruct((4, SEQ, SEQ), jnp.bfloat16),
            jax.ShapeDtypeStruct((SEQ, 4 * HEAD), jnp.float32),
        ],
        compiler_params=VMEM,
        cost_estimate=cost(12),
        name="student_forward",
    )(y, projected, projected, projected)


def backward_kernel(has_start, y_ref, q_ref, kv_ref, probs_ref, context_ref, mine_ref, *rest):
    if has_start:
        start_ref, grad_ref, kt, dk, dv = rest
        dk[...] = start_ref[:, :HEAD]
        dv[...] = start_ref[:, HEAD:]
    else:
        theirs_ref, grad_ref, gkv_ref, kt, dk, dv = rest
        dk[...] = jnp.zeros_like(dk)
        dv[...] = jnp.zeros_like(dv)
    y = y_ref[0]
    kt[...] = kv_ref[:, :HEAD].T

    def store(at, block, value):
        for which, side in ((0, y), (1, 1 - y)):
            lanes = pl.ds(pl.multiple_of((4 * side + block) * HEAD, HEAD), HEAD)
            grad_ref[at, lanes] = value[:, which * HEAD : which * HEAD + HEAD]

    for number in range(SEQ // BLOCK):
        first = number * BLOCK
        limit = first + BLOCK
        parts = parts_of(number)
        for head in range(2):
            cols = slice(head * HEAD, head * HEAD + HEAD)
            queries = q_ref[first:limit, cols]
            target = mine_ref[0, first:limit, cols].astype(jnp.float32)
            if not has_start:
                target += theirs_ref[first:limit, cols].astype(jnp.float32)
            incoming = ((context_ref[first:limit, cols] - target) * (1.0 / 16)).astype(
                jnp.bfloat16
            )
            rounded = [probs_ref[head, lo:hi, first:limit] for lo, hi in parts]
            probs = [r.astype(jnp.float32) for r in rounded]
            grad_probs = [
                lax.dot_general(
                    kv_ref[lo:hi, HEAD:], incoming, NT, preferred_element_type=jnp.float32
                )
                for lo, hi in parts
            ]
            inner = sum(
                jnp.sum(g * p, axis=0, keepdims=True) for g, p in zip(grad_probs, probs)
            )
            scaled = [
                (p * (g - inner)).astype(jnp.bfloat16) for g, p in zip(grad_probs, probs)
            ]
            for r, s, (lo, hi) in zip(rounded, scaled, parts):
                dv[lo:hi, :] += dot(r, incoming)
                dk[lo:hi, :] += dot(s, queries)
            grad = sum(dot(kt[:, lo:hi], s) for s, (lo, hi) in zip(scaled, parts))
            store(cols, number, (grad * FACTOR).astype(jnp.bfloat16))

    if has_start:
        for number in range(SEQ // BLOCK):
            rows = slice(number * BLOCK, number * BLOCK + BLOCK)
            store(slice(256, 384), number, (dk[rows, :] * FACTOR).T.astype(jnp.bfloat16))
            store(slice(384, 512), number, dv[rows, :].T.astype(jnp.bfloat16))
    else:
        gkv_ref[:, :HEAD] = dk[...]
        gkv_ref[:, HEAD:] = dv[...]


def student_backward(y, forward, mine, part, theirs=None, start=None):
    queries, kv, probs, context = forward
    pair = pl.BlockSpec((SEQ, 2 * HEAD), lambda i, y: (0, part))
    whole = pl.BlockSpec((SEQ, 2 * HEAD), lambda i, y: (0, 0))
    columns = 256 if start is None else 512
    grad = pl.BlockSpec((columns, SEQ), lambda i, y: (0, 0))
    grad_shape = jax.ShapeDtypeStruct((columns, SEQ), jnp.bfloat16)
    target = (lambda i, y: (y[0], 0, 0)) if start is None else (lambda i, y: (0, 0, 0))
    return pl.pallas_call(
        lambda *refs: backward_kernel(start is not None, *refs),
        grid_spec=pltpu.PrefetchScalarGridSpec(
            num_scalar_prefetch=1,
            grid=(1,),
            in_specs=[
                pair,
                whole,
                pl.BlockSpec((2, SEQ, SEQ), lambda i, y: (part, 0, 0)),
                pair,
                pl.BlockSpec((1, SEQ, 2 * HEAD), target),
                whole,
            ],
            out_specs=[grad, whole] if start is None else [grad],
            scratch_shapes=[
                pltpu.VMEM((HEAD, SEQ), jnp.bfloat16),
                pltpu.VMEM((SEQ, HEAD), jnp.float32),
                pltpu.VMEM((SEQ, HEAD), jnp.float32),
            ],
        ),
        out_shape=[grad_shape, jax.ShapeDtypeStruct((SEQ, 2 * HEAD), jnp.float32)]
        if start is None
        else [grad_shape],
        compiler_params=VMEM,
        cost_estimate=cost(8),
        name="student_backward",
    )(y, queries, kv, probs, context, mine, theirs if start is None else start)


def shift(array, axis, step=1):
    n = lax.axis_size(axis)
    return lax.ppermute(array, axis, [(i, (i + step) % n) for i in range(n)])


def gather_rows_near(own):
    return shift(own, "yhi"), shift(own, "x", 1), shift(own, "x", -1)


def far_halves(left, right):
    half = left.shape[0] // 2
    return shift(left[:half], "x", 1), shift(right[half:], "x", -1)


def row_places(x):
    places = [(x + dx) % 4 * 128 + offset for dx, offset in ((0, 0), (3, 0), (1, 0), (2, 0), (2, 64))]
    return jnp.stack(places).astype(jnp.int32)


RELATIVE = [(dy, dz) for dy in range(2) for dz in range(4)]


def row_blocks():
    y = lax.axis_index("ylo")
    z = lax.axis_index("z")
    return jnp.stack([(y + dy) % 2 * 4 + (z + dz) % 4 for dy, dz in RELATIVE]).astype(jnp.int32)


def send_direct(blocks):
    got = [blocks[0]]
    for (dy, dz), block in zip(RELATIVE[1:], blocks[1:]):
        route = [(i * 4 + k, (i + dy) % 2 * 4 + (k + dz) % 4) for i in range(2) for k in range(4)]
        got.append(lax.ppermute(block, ("ylo", "z"), route))
    return got


def finish_kernel(*refs):
    a_refs, b_refs, (q_ref, k_ref, v_ref) = refs[:2], refs[2:10], refs[10:]

    def total(parts):
        result = parts[0][...].astype(jnp.float32)
        for part in parts[1:]:
            result += part[...].astype(jnp.float32)
        return result.T

    q_ref[:, :256] = total(a_refs)
    rest = total(b_refs)
    q_ref[:, 256:] = rest[:, :256]
    k_ref[...] = rest[:, 256:384]
    v_ref[...] = rest[:, 384:]


def finish(got_a, got_b):
    return pl.pallas_call(
        finish_kernel,
        out_shape=[jax.ShapeDtypeStruct((256, cols), jnp.float32) for cols in (512, 128, 128)],
        compiler_params=VMEM,
        cost_estimate=cost(3),
        name="finish",
    )(*got_a, *got_b)


def per_device(
    teacher_queries,
    teacher_keys,
    teacher_values,
    projector,
    student_inputs,
    query_weight,
    key_weight,
    value_weight,
):
    tq, tk, tv = teacher_queries[0], teacher_keys[0], teacher_values[0]
    x, yhi, ylo = lax.axis_index("x"), lax.axis_index("yhi"), lax.axis_index("ylo")
    own = student_inputs[0]
    other, left, right = gather_rows_near(own)
    shard = jnp.concatenate([query_weight, key_weight, value_weight], axis=1)

    groups = jnp.arange(4, dtype=jnp.int32)
    context = teacher_attention(tq, tk, tv, 0)
    near = lax.all_gather(shard, ("z", "core"), axis=0, tiled=True)
    shard_far = shift(shard, "ylo")
    context, left, right, other, shard_far = lax.optimization_barrier(
        (context, left, right, other, shard_far)
    )
    context = teacher_attention(tq, tk, tv, 1, (context,))
    sent = project(2 * (2 * groups + 1 - yhi) + 1, context, projector, 1)
    far = lax.all_gather(shard_far, ("z", "core"), axis=0, tiled=True)
    came = shift(sent, "yhi")
    product_a = project(2 * jnp.arange(8, dtype=jnp.int32), context, projector, 1)
    sum_a = lax.psum_scatter(product_a, "x", scatter_dimension=0, tiled=True)

    own_far = far_halves(left, right)
    other_left, other_right = shift(other, "x", 1), shift(other, "x", -1)
    context, other_left, other_right, own_far, near, far = lax.optimization_barrier(
        (context, other_left, other_right, own_far, near, far)
    )
    kept = project(2 * (2 * groups + yhi) + 1, context, projector, 150)
    other_far = far_halves(other_left, other_right)

    places = row_places(x)
    order = jnp.stack([2 * ylo, 2 * ylo + 1, 2 - 2 * ylo, 3 - 2 * ylo]).astype(jnp.int32)
    before = student_project(places, order, [own, left, right, *own_far], near, far)
    came, before, *other_far = lax.optimization_barrier((came, before, *other_far))
    both = (kept.astype(jnp.float32) + came.astype(jnp.float32)).astype(jnp.bfloat16)
    sum_b = lax.psum_scatter(both, "x", scatter_dimension=0, tiled=True)
    projected, rows = student_project(
        places, order, [other, other_left, other_right, *other_far], near, far, before
    )

    y = yhi.astype(jnp.int32).reshape(1)
    theirs_a = shift(lax.dynamic_index_in_dim(sum_a, 1 - yhi, 0, keepdims=False), "yhi")
    core = lax.axis_index("core").astype(jnp.int32).reshape(1)
    forward = student_forward(y, projected)
    forward, theirs_a = lax.optimization_barrier((forward, theirs_a))

    grad_a, part_kv = student_backward(y, forward, sum_a, 0, theirs=theirs_a)
    whole_a = weight_grad_ring(grad_a, rows)
    ring_a = lax.psum_scatter(
        whole_a.reshape(16, 256, 256), ("z", "core"), scatter_dimension=0, tiled=True
    )
    sum_b, whole_a = lax.optimization_barrier((sum_b, whole_a))
    (grad_b,) = student_backward(y, forward, sum_b, 1, start=part_kv)
    kept_b, sent_b = weight_grad(core, row_blocks(), grad_b, rows)
    got_b = send_direct(list(pair_sum(kept_b, shift(sent_b, "core"))))
    theirs = shift(lax.dynamic_index_in_dim(ring_a, 1 - ylo, 0, keepdims=False), "ylo")
    mine = lax.dynamic_index_in_dim(ring_a, ylo, 0, keepdims=False)
    return tuple(finish([mine, theirs], got_b))


def solution(mesh):
    fine = Mesh(mesh.devices.reshape(2, 4, 2, 4, 2), DP + TENSOR)
    placed = (
        P(DP, None, TENSOR),
        P(DP, None, TENSOR),
        P(DP, None, TENSOR),
        P(TENSOR, None),
        P(DP, TENSOR, None),
        P(DP, TENSOR),
        P(DP, TENSOR),
        P(DP, TENSOR),
    )
    return jax.shard_map(
        per_device,
        mesh=fine,
        in_specs=placed,
        out_specs=(P(DP, TENSOR), P(DP, TENSOR), P(DP, TENSOR)),
        check_vma=False,
    )
```

time: 310 us -> 255 us (0.82); the launches traced: 305 us -> 254 us
  waiting for transfers between devices: 114 us -> 56.5 us
  local copies, waits for them, and re-layouts: 31.1 us -> 14 us
  Pallas kernels: 103 us -> 116 us
  starting transfers between devices: 37.8 us -> 46.1 us
    ppermute x14 -> x7, waiting for transfers between devices: 34 us -> 8.32 us  [send_direct(): got.append(lax.ppermute(block, ('ylo', 'z'), route))]
    unnamed x82 -> x32, local copies, waits for them, and re-layouts: 27.9 us -> 5.39 us
    ppermute x13 -> x14, waiting for transfers between devices: 64.7 us -> 44.8 us  [shift(): return lax.ppermute(array, axis, [(i, (i + step) % n) for i in range(n)])]
    all_gather x1 -> x2, waiting for transfers between devices: 11.2 us -> 0.04 us  [the longest x1 0.02 us: per_device(): near = lax.all_gather(shard, ('z', 'core'), axis=0, tiled=True)]
    ppermute x14 -> x7, starting transfers between devices: 16 us -> 26 us  [send_direct(): got.append(lax.ppermute(block, ('ylo', 'z'), route))]
    pallas_call x9, Pallas kernels: 79.3 us -> 85.2 us  [the longest x2 19.7 us: student_project(): pl.pallas_call(lambda *refs: student_project_kernel(count, *refs), grid_s...]
    pallas_call x3, Pallas kernels: 20 us -> 24.2 us  [project(): pl.pallas_call(project_kernel, grid_spec=pltpu.PrefetchScalarGridSpec(num...]
    ppermute x13 -> x14, starting transfers between devices: 21.6 us -> 19.9 us  [shift(): return lax.ppermute(array, axis, [(i, (i + step) % n) for i in range(n)])]
  transfers between devices with their start and end apart: 30 -> 26, of which waited for: 9 -> 10; matrix products, arithmetic and copies ran while one was open for 2% -> 5% of each run, Pallas kernels for 27% -> 44%
where the time goes in v3:
time: 255 us; the launch traced here: 254 us
  Pallas kernels  116 us (45%)
  waiting for transfers between devices  56.5 us (22%)
  starting transfers between devices  46.1 us (18%)
  between operations  15.9 us (6%)
  local copies, waits for them, and re-layouts  14 us (5%)
  other arithmetic  5.77 us (2%)
    ppermute x14, waiting for transfers between devices, shift(): return lax.ppermute(array, axis, [(i, (i + step) % n) for i in range(n)])  44.8 us
    ppermute x7, starting transfers between devices, send_direct(): got.append(lax.ppermute(block, ('ylo', 'z'), route))  26 us
    pallas_call x3, Pallas kernels, project(): pl.pallas_call(project_kernel, grid_spec=pltpu.PrefetchScalarGridSpec(num...  24.2 us
    ppermute x14, starting transfers between devices, shift(): return lax.ppermute(array, axis, [(i, (i + step) % n) for i in range(n)])  19.9 us
    pallas_call x2, Pallas kernels, student_project(): pl.pallas_call(lambda *refs: student_project_kernel(count, *refs), grid_s...  19.7 us
    pallas_call x2, Pallas kernels, teacher_attention(): pl.pallas_call(lambda q_ref, k_ref, v_ref, *rest: teacher_kernel(q_ref, k...  16.8 us
    pallas_call x2, Pallas kernels, student_backward(): pl.pallas_call(lambda *refs: backward_kernel(start is not None, *refs), g...  16.7 us
    pallas_call x1, Pallas kernels, weight_grad(): pl.pallas_call(weight_grad_kernel, grid_spec=pltpu.PrefetchScalarGridSpec...  11.5 us
  transfers between devices with their start and end apart: 26, of which 10 were waited for; matrix products, arithmetic and copies ran while one was open for 5% of the time, Pallas kernels for 44%

profile of v3, /device:TPU:0, one launch (start us, length us, event | category | flops | bytes accessed | tf_op | source)
XLA Modules:
  0.0 254.0 jit_solution(8566067169702388932)
XLA Ops:
  13.3 2.9 %collective-permute-start.2 = (bf16[128,4096]{1,0:T(8,128)(2,1)}, bf16[128,4096]{1,0:T(8,128)(2,1)}, u32[]{:S(2)}, u32[]{:S(2)}) collective-permute-start(bf16[128,4096]{1,0:T(8,128)(2,1)} %bitcast.37), channel_id=1, source_target_pairs={{0,1},{1,0},{2,3},{3,2},{4,5},{5,4},{6,7},{7,6},{8,9},{9,8},{10,11... | collective-permute-start | bytes 3145736 | tf_op jit(solution)/shard_map/ppermute | solution.py:411
  16.2 2.8 %collective-permute-start.1 = (bf16[128,4096]{1,0:T(8,128)(2,1)}, bf16[128,4096]{1,0:T(8,128)(2,1)}, u32[]{:S(2)}, u32[]{:S(2)}) collective-permute-start(bf16[128,4096]{1,0:T(8,128)(2,1)} %bitcast.38), channel_id=1, source_target_pairs={{0,6},{2,0},{4,2},{6,4},{1,7},{3,1},{5,3},{7,5},{8,14},{10,8},{12,... | collective-permute-start | bytes 3145736 | tf_op jit(solution)/shard_map/ppermute | solution.py:411
  19.0 8.4 %teacher_attention.2.rest_0_ = bf16[1024,1024]{1,0:T(8,128)(2,1)} custom-call(bf16[1024,1024]{1,0:T(8,128)(2,1)} %bitcast.30, bf16[1024,128]{1,0:T(8,128)(2,1)} %bitcast.33, bf16[1024,128]{1,0:T(8,128)(2,1)} %bitcast.35), custom_call_target="tpu_custom_call" | custom-call | flops 40000000000 | tf_op jit(solution)/shard_map/teacher_attention/pallas_call | solution.py:65
  27.4 20.5 %collective-permute-done.2.refs_2_ = bf16[128,4096]{1,0:T(8,128)(2,1)} collective-permute-done((bf16[128,4096]{1,0:T(8,128)(2,1)}, bf16[128,4096]{1,0:T(8,128)(2,1)}, u32[]{:S(2)}, u32[]{:S(2)}) %collective-permute-start.2) | collective-permute-done | bytes 1048608 | tf_op jit(solution)/shard_map/ppermute | solution.py:411
  47.9 2.8 %collective-permute-start.5 = (bf16[128,4096]{1,0:T(8,128)(2,1)}, bf16[128,4096]{1,0:T(8,128)(2,1)S(1)}, u32[]{:S(2)}, u32[]{:S(2)}) collective-permute-start(bf16[128,4096]{1,0:T(8,128)(2,1)} %collective-permute-done.2.refs_2_), channel_id=1, source_target_pairs={{0,6},{2,0},{4,2},{6,4},{1,7},{3,1},{5,3},{7,5},{8,14},{10,8},{12,... | collective-permute-start | bytes 3145736 | tf_op jit(solution)/shard_map/ppermute | solution.py:411
  53.5 3.3 %collective-permute-start.7 = (bf16[64,4096]{1,0:T(8,128)(2,1)S(1)}, bf16[64,4096]{1,0:T(8,128)(2,1)}, u32[]{:S(2)}, u32[]{:S(2)}) collective-permute-start(bf16[64,4096]{1,0:T(8,128)(2,1)S(1)} %slice.13), channel_id=1, source_target_pairs={{0,6},{2,0},{4,2},{6,4},{1,7},{3,1},{5,3},{7,5},{8,14},{10,8},{12,... | collective-permute-start | bytes 1572872 | tf_op jit(solution)/shard_map/ppermute | solution.py:411
  59.1 8.4 %teacher_attention.3.context_ref = bf16[1024,1024]{1,0:T(8,128)(2,1)} custom-call(bf16[1024,1024]{1,0:T(8,128)(2,1)} %bitcast.31, bf16[1024,128]{1,0:T(8,128)(2,1)} %bitcast.34, bf16[1024,128]{1,0:T(8,128)(2,1)} %bitcast.36, bf16[1024,1024]{1,0:T(8,128)(2,1)} %teacher_attention.2.rest_0_), custom_call_target="tpu_custom_call", output_to_operand_aliasing={{}: (3, {})} | custom-call | flops 1000000000 | tf_op jit(solution)/shard_map/teacher_attention/pallas_call | solution.py:65
  67.5 6.8 %project.3 = bf16[4,1024,256]{2,1,0:T(8,128)(2,1)} custom-call(s32[4]{0:T(128)} %multiply_add_fusion.1.order_ref, bf16[1024,1024]{1,0:T(8,128)(2,1)} %teacher_attention.3.context_ref, bf16[1024,4096]{1,0:T(8,128)(2,1)} %p_ref.5), custom_call_target="tpu_custom_call" | custom-call | flops 1000000000 | tf_op jit(solution)/shard_map/project/pallas_call | solution.py:85
  75.0 10.7 %project.4 = bf16[8,1024,256]{2,1,0:T(8,128)(2,1)} custom-call(s32[8]{0:T(128)} %iota_multiply_fusion.order_ref, bf16[1024,1024]{1,0:T(8,128)(2,1)} %teacher_attention.3.context_ref, bf16[1024,4096]{1,0:T(8,128)(2,1)} %p_ref.5), custom_call_target="tpu_custom_call" | custom-call | flops 1000000000 | tf_op jit(solution)/shard_map/project/pallas_call | solution.py:85
  91.1 6.7 %project.5 = bf16[4,1024,256]{2,1,0:T(8,128)(2,1)} custom-call(s32[4]{0:T(128)} %multiply_add_fusion.order_ref, bf16[1024,1024]{1,0:T(8,128)(2,1)} %teacher_attention.3.context_ref, bf16[1024,4096]{1,0:T(8,128)(2,1)} %p_ref.5), custom_call_target="tpu_custom_call" | custom-call | flops 149999992832 | tf_op jit(solution)/shard_map/project/pallas_call | solution.py:85
  97.8 9.9 %student_project.2 = (bf16[1024,768]{1,0:T(8,128)(2,1)}, bf16[1024,4096]{1,0:T(8,128)(2,1)}) custom-call(s32[5]{0:T(128)} %stack.65.refs_0_, s32[4]{0:T(128)} %pad_add_fusion.refs_1_, bf16[128,4096]{1,0:T(8,128)(2,1)} %bitcast.40, bf16[128,4096]{1,0:T(8,128)(2,1)} %collective-permute-done.refs_3_, bf16[128,4096]{1,0:T(8,128)(2,1)} %collective-permute-done.1.refs_4_, ...), custom_call_target="tpu_custom_call" | custom-call | flops 8999999488 | tf_op jit(solution)/shard_map/student_project/pallas_call | solution.py:133
  107.7 14.0 %collective-permute-done.8 = bf16[4,1024,256]{2,1,0:T(8,128)(2,1)} collective-permute-done((bf16[4,1024,256]{2,1,0:T(8,128)(2,1)}, bf16[4,1024,256]{2,1,0:T(8,128)(2,1)}, u32[]{:S(2)}, u32[]{:S(2)}) %collective-permute-start.8) | collective-permute-done | bytes 2097184 | tf_op jit(solution)/shard_map/ppermute | solution.py:411
  121.8 3.4 %add_convert_fusion = bf16[4,1024,256]{2,1,0:T(8,128)(2,1)} fusion(bf16[4,1024,256]{2,1,0:T(8,128)(2,1)} %collective-permute-done.8, bf16[4,1024,256]{2,1,0:T(8,128)(2,1)S(1)} %copy-done), kind=kLoop, calls=%fused_computation | loop fusion | flops 4194304 | bytes 6291456 | tf_op jit(solution)/shard_map/convert_element_type | solution.py:513
  125.3 9.8 %student_project.3 = (bf16[1024,768]{1,0:T(8,128)(2,1)}, bf16[1024,4096]{1,0:T(8,128)(2,1)}) custom-call(s32[5]{0:T(128)} %stack.65.refs_0_, s32[4]{0:T(128)} %pad_add_fusion.refs_1_, bf16[128,4096]{1,0:T(8,128)(2,1)} %collective-permute-done.2.refs_2_, bf16[128,4096]{1,0:T(8,128)(2,1)} %copy-done.4, ...), custom_call_target="tpu_custom_call", output_to_operand_aliasing={{0}: (9, {}), {1}: (10, {})} | custom-call | flops 8999999488 | tf_op jit(solution)/shard_map/student_project/pallas_call | solution.py:133
  135.1 3.3 %reduce-scatter.4.cloned.1.call-done.refs_5_ = bf16[2,1024,256]{2,1,0:T(8,128)(2,1)} async-done(((bf16[8,1024,256]{2,1,0:T(8,128)(2,1)}), bf16[2,1024,256]{2,1,0:T(8,128)(2,1)}) %reduce-scatter.4.cloned.1.call-update) | async-done | bytes 1048592 | tf_op jit(solution)/shard_map/reduce_scatter | solution.py:499
  139.4 3.2 %collective-permute-start.11 = (bf16[1024,256]{1,0:T(8,128)(2,1)S(1)}, bf16[1024,256]{1,0:T(8,128)(2,1)S(1)}, u32[]{:S(2)}, u32[]{:S(2)}) collective-permute-start(bf16[1024,256]{1,0:T(8,128)(2,1)S(1)} %dynamic-slice_bitcast_fusion), channel_id=1, source_target_pairs={{0,1},{1,0},{2,3},{3,2},{4,5},{5,4},{6,7},{7,6},{8,9},{9,8},{10,11... | collective-permute-start | bytes 1572872 | tf_op jit(solution)/shard_map/ppermute | solution.py:411
  142.6 11.1 %student_forward.1 = (bf16[1024,512]{1,0:T(8,128)(2,1)}, bf16[1024,256]{1,0:T(8,128)(2,1)}, bf16[4,1024,1024]{2,1,0:T(8,128)(2,1)}, f32[1024,512]{1,0:T(8,128)}) custom-call(s32[1]{0:T(128)} %bitcast.y_ref.refs_0_, bf16[1024,768]{1,0:T(8,128)(2,1)} %get-tuple-element.63.q_in.k_in.v_in, bf16[1024,768]{1,0:T(8,128)(2,1)} %get-tuple-element.63.q_in.k_in.v_in, ...), custom_call_target="tpu_custom_call" | custom-call | flops 12000000000 | tf_op jit(solution)/shard_map/student_forward/pallas_call | solution.py:287
  155.9 8.3 %student_backward.2 = (bf16[256,1024]{1,0:T(8,128)(2,1)}, f32[1024,256]{1,0:T(8,128)}) custom-call(s32[1]{0:T(128)} %bitcast.y_ref.refs_0_, bf16[1024,512]{1,0:T(8,128)(2,1)} %get-tuple-element.68.refs_1_, bf16[1024,256]{1,0:T(8,128)(2,1)} %get-tuple-element.69.refs_2_, bf16[4,1024,1024]{2,1,0:T(8,128)(2,1)} %get-tuple-element.70.refs_3_, ...), custom_call_target="tpu_custom_call" | custom-call | flops 8000000000 | tf_op jit(solution)/shard_map/student_backward/pallas_call | solution.py:380
  164.2 9.4 %weight_grad_ring.1 = bf16[4,2,2,256,256]{4,3,2,1,0:T(8,128)(2,1)} custom-call(s32[8]{0:T(128)} %constant.119.clone.order_ref, bf16[256,1024]{1,0:T(8,128)(2,1)} %get-tuple-element.73.grad_ref, bf16[1024,4096]{1,0:T(8,128)(2,1)} %get-tuple-element.74.rows_ref), custom_call_target="tpu_custom_call" | custom-call | flops 4000000000 | tf_op jit(solution)/shard_map/weight_grad_ring/pallas_call | solution.py:173
  174.3 8.4 %student_backward.3.grad_ref = bf16[512,1024]{1,0:T(8,128)(2,1)} custom-call(s32[1]{0:T(128)} %bitcast.y_ref.refs_0_, bf16[1024,512]{1,0:T(8,128)(2,1)} %get-tuple-element.68.refs_1_, bf16[1024,256]{1,0:T(8,128)(2,1)} %get-tuple-element.69.refs_2_, bf16[4,1024,1024]{2,1,0:T(8,128)(2,1)} %get-tuple-element.70.refs_3_, f32[1024,512]{1,0:T(8,128)} %get-tuple-element.71.refs_4_, ...), custom_call_target="tpu_custom_call" | custom-call | flops 8000000000 | tf_op jit(solution)/shard_map/student_backward/pallas_call | solution.py:380
  182.7 11.5 %weight_grad.1 = (bf16[8,512,256]{2,1,0:T(8,128)(2,1)}, bf16[8,512,256]{2,1,0:T(8,128)(2,1)}) custom-call(s32[1]{0:T(128)} %bitcast.18.core_ref, s32[8]{0:T(128)} %stack.79.order_ref, bf16[512,1024]{1,0:T(8,128)(2,1)} %student_backward.3.grad_ref, bf16[1024,4096]{1,0:T(8,128)(2,1)} %get-tuple-element.74.rows_ref), custom_call_target="tpu_custom_call" | custom-call | flops 4000000000 | tf_op jit(solution)/shard_map/weight_grad/pallas_call | solution.py:210
  194.2 4.4 %collective-permute-done.13.b_ref = bf16[8,512,256]{2,1,0:T(8,128)(2,1)S(1)} collective-permute-done((bf16[8,512,256]{2,1,0:T(8,128)(2,1)}, bf16[8,512,256]{2,1,0:T(8,128)(2,1)S(1)}, u32[]{:S(2)}, u32[]{:S(2)}) %collective-permute-start.13) | collective-permute-done | bytes 2097184 | tf_op jit(solution)/shard_map/ppermute | solution.py:411
  199.9 3.7 %pair_sum.1 = (bf16[512,256]{1,0:T(8,128)(2,1)}, bf16[512,256]{1,0:T(8,128)(2,1)}, bf16[512,256]{1,0:T(8,128)(2,1)}, bf16[512,256]{1,0:T(8,128)(2,1)}, bf16[512,...) custom-call(bf16[8,512,256]{2,1,0:T(8,128)(2,1)} %get-tuple-element.79.a_ref, ...), custom_call_target="tpu_custom_call" | custom-call | flops 3000000000 | tf_op jit(solution)/shard_map/pair_sum/pallas_call | solution.py:236
  203.6 2.0 collective-permute-start.14
  205.6 3.6 %collective-permute-start.15 = (bf16[512,256]{1,0:T(8,128)(2,1)}, bf16[512,256]{1,0:T(8,128)(2,1)S(1)}, u32[]{:S(2)}, u32[]{:S(2)}) collective-permute-start(bf16[512,256]{1,0:T(8,128)(2,1)} %get-tuple-element.83), channel_id=1, source_target_pairs={{0,32},{16,48},{32,0},{48,16},{64,96},{80,112},{96,64},{112,80},{1... | collective-permute-start | bytes 786440 | tf_op jit(solution)/shard_map/ppermute | solution.py:441
  210.6 2.1 collective-permute-start.18
  212.7 1.9 collective-permute-done.14.refs_3_
  214.6 15.4 %collective-permute-start.19 = (bf16[512,256]{1,0:T(8,128)(2,1)}, bf16[512,256]{1,0:T(8,128)(2,1)S(1)}, u32[]{:S(2)}, u32[]{:S(2)}) collective-permute-start(bf16[512,256]{1,0:T(8,128)(2,1)} %get-tuple-element.87), channel_id=1, source_target_pairs={{0,96},{16,112},{32,64},{48,80},{64,32},{80,48},{96,0},{112,16},{1... | collective-permute-start | bytes 786440 | tf_op jit(solution)/shard_map/ppermute | solution.py:441
  233.6 3.5 %collective-permute-done.19.refs_8_ = bf16[512,256]{1,0:T(8,128)(2,1)S(1)} collective-permute-done((bf16[512,256]{1,0:T(8,128)(2,1)}, bf16[512,256]{1,0:T(8,128)(2,1)S(1)}, u32[]{:S(2)}, u32[]{:S(2)}) %collective-permute-start.19) | collective-permute-done | bytes 262176 | tf_op jit(solution)/shard_map/ppermute | solution.py:441
  237.1 2.9 %collective-permute-done.20.refs_9_ = bf16[512,256]{1,0:T(8,128)(2,1)S(1)} collective-permute-done((bf16[512,256]{1,0:T(8,128)(2,1)}, bf16[512,256]{1,0:T(8,128)(2,1)S(1)}, u32[]{:S(2)}, u32[]{:S(2)}) %collective-permute-start.20) | collective-permute-done | bytes 262176 | tf_op jit(solution)/shard_map/ppermute | solution.py:441
  240.0 3.0 %collective-permute-done.12.refs_1_ = bf16[256,256]{1,0:T(8,128)(2,1)S(1)} collective-permute-done((bf16[256,256]{1,0:T(8,128)(2,1)S(1)}, bf16[256,256]{1,0:T(8,128)(2,1)S(1)}, u32[]{:S(2)}, u32[]{:S(2)}) %collective-permute-start.12) | collective-permute-done | bytes 131104 | tf_op jit(solution)/shard_map/ppermute | solution.py:411
  243.7 2.7 %finish.1 = (f32[256,512]{1,0:T(8,128)}, f32[256,128]{1,0:T(8,128)}, f32[256,128]{1,0:T(8,128)}) custom-call(bf16[256,256]{1,0:T(8,128)(2,1)} %get-tuple-element.90.refs_0_, bf16[256,256]{1,0:T(8,128)(2,1)} %copy-done.14, bf16[512,256]{1,0:T(8,128)(2,1)} %get-tuple-element.81.refs_2_, bf16[512,256]{1,0:T(8,128)(2,1)} %copy-done.7, ...), custom_call_target="tpu_custom_call" | custom-call | flops 3000000000 | tf_op jit(solution)/shard_map/finish/pallas_call | solution.py:462
  (85 shorter events, 27.4 us)
Async XLA Ops:
  8.0 79.3 %all-gather.3.cloned.1.call-start = ((), (), s32[]{:S(2)}) async-start(), calls=%async_computation.3 | async-start | bytes 3538944 | tf_op jit(solution)/shard_map/all_gather | solution.py:489
  11.5 75.8 %all-gather.5.cloned.1.call-start = ((), (), s32[]{:S(2)}) async-start(), calls=%async_computation.4 | async-start | bytes 3538944 | tf_op jit(solution)/shard_map/all_gather | solution.py:496
  11.6 15.8 %collective-permute-start.3 = (bf16[256,768]{1,0:T(8,128)(2,1)}, bf16[256,768]{1,0:T(8,128)(2,1)S(1)}, u32[]{:S(2)}, u32[]{:S(2)}) collective-permute-start(bf16[256,768]{1,0:T(8,128)(2,1)} %copy-done.1), channel_id=1, source_target_pairs={{0,64},{64,0},{1,65},{65,1},{2,66},{66,2},{3,67},{67,3},{4,68},{68... | collective-permute-start | bytes 1179656 | tf_op jit(solution)/shard_map/ppermute | solution.py:411
  13.3 34.5 %collective-permute-start.2 = (bf16[128,4096]{1,0:T(8,128)(2,1)}, bf16[128,4096]{1,0:T(8,128)(2,1)}, u32[]{:S(2)}, u32[]{:S(2)}) collective-permute-start(bf16[128,4096]{1,0:T(8,128)(2,1)} %bitcast.37), channel_id=1, source_target_pairs={{0,1},{1,0},{2,3},{3,2},{4,5},{5,4},{6,7},{7,6},{8,9},{9,8},{10,11... | collective-permute-start | bytes 3145736 | tf_op jit(solution)/shard_map/ppermute | solution.py:411
  16.2 31.6 %collective-permute-start.1 = (bf16[128,4096]{1,0:T(8,128)(2,1)}, bf16[128,4096]{1,0:T(8,128)(2,1)}, u32[]{:S(2)}, u32[]{:S(2)}) collective-permute-start(bf16[128,4096]{1,0:T(8,128)(2,1)} %bitcast.38), channel_id=1, source_target_pairs={{0,6},{2,0},{4,2},{6,4},{1,7},{3,1},{5,3},{7,5},{8,14},{10,8},{12,... | collective-permute-start | bytes 3145736 | tf_op jit(solution)/shard_map/ppermute | solution.py:411
  19.0 28.9 %collective-permute-start = (bf16[128,4096]{1,0:T(8,128)(2,1)}, bf16[128,4096]{1,0:T(8,128)(2,1)}, u32[]{:S(2)}, u32[]{:S(2)}) collective-permute-start(bf16[128,4096]{1,0:T(8,128)(2,1)} %bitcast.39), channel_id=1, source_target_pairs={{0,2},{2,4},{4,6},{6,0},{1,3},{3,5},{5,7},{7,1},{8,10},{10,12},{12... | collective-permute-start | bytes 3145736 | tf_op jit(solution)/shard_map/ppermute | solution.py:411
  27.4 20.5 %copy-start.2 = (bf16[256,768]{1,0:T(8,128)(2,1)}, bf16[256,768]{1,0:T(8,128)(2,1)S(1)}, u32[]{:S(2)}) copy-start(bf16[256,768]{1,0:T(8,128)(2,1)S(1)} %collective-permute-done.3) | copy-start | bytes 1179652
  47.9 90.5 %reduce-scatter.4.cloned.1.call-start = ((), (), s32[]{:S(2)}) async-start(), calls=%async_computation.5 | async-start | bytes 5242880 | tf_op jit(solution)/shard_map/reduce_scatter | solution.py:499
  47.9 39.3 %collective-permute-start.5 = (bf16[128,4096]{1,0:T(8,128)(2,1)}, bf16[128,4096]{1,0:T(8,128)(2,1)S(1)}, u32[]{:S(2)}, u32[]{:S(2)}) collective-permute-start(bf16[128,4096]{1,0:T(8,128)(2,1)} %collective-permute-done.2.refs_2_), channel_id=1, source_target_pairs={{0,6},{2,0},{4,2},{6,4},{1,7},{3,1},{5,3},{7,5},{8,14},{10,8},{12,... | collective-permute-start | bytes 3145736 | tf_op jit(solution)/shard_map/ppermute | solution.py:411
  50.7 36.5 %collective-permute-start.4 = (bf16[128,4096]{1,0:T(8,128)(2,1)}, bf16[128,4096]{1,0:T(8,128)(2,1)S(1)}, u32[]{:S(2)}, u32[]{:S(2)}) collective-permute-start(bf16[128,4096]{1,0:T(8,128)(2,1)} %collective-permute-done.2.refs_2_), channel_id=1, source_target_pairs={{0,2},{2,4},{4,6},{6,0},{1,3},{3,5},{5,7},{7,1},{8,10},{10,12},{12... | collective-permute-start | bytes 3145736 | tf_op jit(solution)/shard_map/ppermute | solution.py:411
  53.5 32.3 %collective-permute-start.7 = (bf16[64,4096]{1,0:T(8,128)(2,1)S(1)}, bf16[64,4096]{1,0:T(8,128)(2,1)}, u32[]{:S(2)}, u32[]{:S(2)}) collective-permute-start(bf16[64,4096]{1,0:T(8,128)(2,1)S(1)} %slice.13), channel_id=1, source_target_pairs={{0,6},{2,0},{4,2},{6,4},{1,7},{3,1},{5,3},{7,5},{8,14},{10,8},{12,... | collective-permute-start | bytes 1572872 | tf_op jit(solution)/shard_map/ppermute | solution.py:411
  56.8 30.5 %collective-permute-start.6 = (bf16[64,4096]{1,0:T(8,128)(2,1)S(1)}, bf16[64,4096]{1,0:T(8,128)(2,1)}, u32[]{:S(2)}, u32[]{:S(2)}) collective-permute-start(bf16[64,4096]{1,0:T(8,128)(2,1)S(1)} %slice.12), channel_id=1, source_target_pairs={{0,2},{2,4},{4,6},{6,0},{1,3},{3,5},{5,7},{7,1},{8,10},{10,12},{12... | collective-permute-start | bytes 1572872 | tf_op jit(solution)/shard_map/ppermute | solution.py:411
  74.3 47.5 %collective-permute-start.8 = (bf16[4,1024,256]{2,1,0:T(8,128)(2,1)}, bf16[4,1024,256]{2,1,0:T(8,128)(2,1)}, u32[]{:S(2)}, u32[]{:S(2)}) collective-permute-start(bf16[4,1024,256]{2,1,0:T(8,128)(2,1)} %project.3), channel_id=1, source_target_pairs={{0,1},{1,0},{2,3},{3,2},{4,5},{5,4},{6,7},{7,6},{8,9},{9,8},{10,11... | collective-permute-start | bytes 6291464 | tf_op jit(solution)/shard_map/ppermute | solution.py:411
  85.7 88.6 %reduce-scatter.8.cloned.1.call-start = ((), (), s32[]{:S(2)}) async-start(), calls=%async_computation.7 | async-start | bytes 2621440 | tf_op jit(solution)/shard_map/reduce_scatter | solution.py:514
  87.3 10.6 %copy-start.4 = (bf16[128,4096]{1,0:T(8,128)(2,1)}, bf16[128,4096]{1,0:T(8,128)(2,1)S(1)}, u32[]{:S(2)}) copy-start(bf16[128,4096]{1,0:T(8,128)(2,1)S(1)} %collective-permute-done.4.refs_3_) | copy-start | bytes 3145732
  89.1 32.7 %collective-permute-start.10 = (bf16[64,4096]{1,0:T(8,128)(2,1)}, bf16[64,4096]{1,0:T(8,128)(2,1)}, u32[]{:S(2)}, u32[]{:S(2)}) collective-permute-start(bf16[64,4096]{1,0:T(8,128)(2,1)} %slice.15), channel_id=1, source_target_pairs={{0,6},{2,0},{4,2},{6,4},{1,7},{3,1},{5,3},{7,5},{8,14},{10,8},{12,... | collective-permute-start | bytes 1572872 | tf_op jit(solution)/shard_map/ppermute | solution.py:411
  90.8 30.9 %collective-permute-start.9 = (bf16[64,4096]{1,0:T(8,128)(2,1)}, bf16[64,4096]{1,0:T(8,128)(2,1)}, u32[]{:S(2)}, u32[]{:S(2)}) collective-permute-start(bf16[64,4096]{1,0:T(8,128)(2,1)} %slice.14), channel_id=1, source_target_pairs={{0,2},{2,4},{4,6},{6,0},{1,3},{3,5},{5,7},{7,1},{8,10},{10,12},{12... | collective-permute-start | bytes 1572872 | tf_op jit(solution)/shard_map/ppermute | solution.py:411
  97.8 24.0 %copy-start = (bf16[4,1024,256]{2,1,0:T(8,128)(2,1)S(1)}, bf16[4,1024,256]{2,1,0:T(8,128)(2,1)}, u32[]{:S(2)}) copy-start(bf16[4,1024,256]{2,1,0:T(8,128)(2,1)} %project.5) | copy-start | bytes 6291460
  125.2 106.3 %reduce-scatter.6.cloned.1.call-start = ((), (), s32[]{:S(2)}) async-start(), calls=%async_computation.6 | async-start | bytes 2359296 | tf_op jit(solution)/shard_map/reduce_scatter | solution.py:527
  139.4 15.7 %collective-permute-start.11 = (bf16[1024,256]{1,0:T(8,128)(2,1)S(1)}, bf16[1024,256]{1,0:T(8,128)(2,1)S(1)}, u32[]{:S(2)}, u32[]{:S(2)}) collective-permute-start(bf16[1024,256]{1,0:T(8,128)(2,1)S(1)} %dynamic-slice_bitcast_fusion), channel_id=1, source_target_pairs={{0,1},{1,0},{2,3},{3,2},{4,5},{5,4},{6,7},{7,6},{8,9},{9,8},{10,11... | collective-permute-start | bytes 1572872 | tf_op jit(solution)/shard_map/ppermute | solution.py:411
  194.2 4.4 %collective-permute-start.13 = (bf16[8,512,256]{2,1,0:T(8,128)(2,1)}, bf16[8,512,256]{2,1,0:T(8,128)(2,1)S(1)}, u32[]{:S(2)}, u32[]{:S(2)}) collective-permute-start(bf16[8,512,256]{2,1,0:T(8,128)(2,1)} %get-tuple-element.80), channel_id=1, source_target_pairs={{0,8},{8,0},{1,9},{9,1},{2,10},{10,2},{3,11},{11,3},{4,12},{12,4},... | collective-permute-start | bytes 6291464 | tf_op jit(solution)/shard_map/ppermute | solution.py:411
  203.6 10.9 %collective-permute-start.14 = (bf16[512,256]{1,0:T(8,128)(2,1)}, bf16[512,256]{1,0:T(8,128)(2,1)S(1)}, u32[]{:S(2)}, u32[]{:S(2)}) collective-permute-start(bf16[512,256]{1,0:T(8,128)(2,1)} %get-tuple-element.82), channel_id=1, source_target_pairs={{0,16},{16,32},{32,48},{48,0},{64,80},{80,96},{96,112},{112,64},{1... | collective-permute-start | bytes 786440 | tf_op jit(solution)/shard_map/ppermute | solution.py:441
  205.6 24.4 %collective-permute-start.15 = (bf16[512,256]{1,0:T(8,128)(2,1)}, bf16[512,256]{1,0:T(8,128)(2,1)S(1)}, u32[]{:S(2)}, u32[]{:S(2)}) collective-permute-start(bf16[512,256]{1,0:T(8,128)(2,1)} %get-tuple-element.83), channel_id=1, source_target_pairs={{0,32},{16,48},{32,0},{48,16},{64,96},{80,112},{96,64},{112,80},{1... | collective-permute-start | bytes 786440 | tf_op jit(solution)/shard_map/ppermute | solution.py:441
  209.2 24.0 %collective-permute-start.16 = (bf16[512,256]{1,0:T(8,128)(2,1)}, bf16[512,256]{1,0:T(8,128)(2,1)S(1)}, u32[]{:S(2)}, u32[]{:S(2)}) collective-permute-start(bf16[512,256]{1,0:T(8,128)(2,1)} %get-tuple-element.84), channel_id=1, source_target_pairs={{0,48},{16,0},{32,16},{48,32},{64,112},{80,64},{96,80},{112,96},{1... | collective-permute-start | bytes 786440 | tf_op jit(solution)/shard_map/ppermute | solution.py:441
  210.4 23.1 %collective-permute-start.17 = (bf16[512,256]{1,0:T(8,128)(2,1)}, bf16[512,256]{1,0:T(8,128)(2,1)S(1)}, u32[]{:S(2)}, u32[]{:S(2)}) collective-permute-start(bf16[512,256]{1,0:T(8,128)(2,1)} %get-tuple-element.85), channel_id=1, source_target_pairs={{0,64},{16,80},{32,96},{48,112},{64,0},{80,16},{96,32},{112,48},{1... | collective-permute-start | bytes 786440 | tf_op jit(solution)/shard_map/ppermute | solution.py:441
  210.6 23.0 %collective-permute-start.18 = (bf16[512,256]{1,0:T(8,128)(2,1)}, bf16[512,256]{1,0:T(8,128)(2,1)S(1)}, u32[]{:S(2)}, u32[]{:S(2)}) collective-permute-start(bf16[512,256]{1,0:T(8,128)(2,1)} %get-tuple-element.86), channel_id=1, source_target_pairs={{0,80},{16,96},{32,112},{48,64},{64,16},{80,32},{96,48},{112,0},{1... | collective-permute-start | bytes 786440 | tf_op jit(solution)/shard_map/ppermute | solution.py:441
  214.6 28.5 %copy-start.7 = (bf16[512,256]{1,0:T(8,128)(2,1)}, bf16[512,256]{1,0:T(8,128)(2,1)S(1)}, u32[]{:S(2)}) copy-start(bf16[512,256]{1,0:T(8,128)(2,1)S(1)} %collective-permute-done.14.refs_3_) | copy-start | bytes 786436
  214.6 22.6 %collective-permute-start.19 = (bf16[512,256]{1,0:T(8,128)(2,1)}, bf16[512,256]{1,0:T(8,128)(2,1)S(1)}, u32[]{:S(2)}, u32[]{:S(2)}) collective-permute-start(bf16[512,256]{1,0:T(8,128)(2,1)} %get-tuple-element.87), channel_id=1, source_target_pairs={{0,96},{16,112},{32,64},{48,80},{64,32},{80,48},{96,0},{112,16},{1... | collective-permute-start | bytes 786440 | tf_op jit(solution)/shard_map/ppermute | solution.py:441
  230.0 13.1 %copy-start.8 = (bf16[512,256]{1,0:T(8,128)(2,1)}, bf16[512,256]{1,0:T(8,128)(2,1)S(1)}, u32[]{:S(2)}) copy-start(bf16[512,256]{1,0:T(8,128)(2,1)S(1)} %collective-permute-done.15.refs_4_) | copy-start | bytes 786436
  230.0 10.1 %collective-permute-start.20 = (bf16[512,256]{1,0:T(8,128)(2,1)}, bf16[512,256]{1,0:T(8,128)(2,1)S(1)}, u32[]{:S(2)}, u32[]{:S(2)}) collective-permute-start(bf16[512,256]{1,0:T(8,128)(2,1)} %get-tuple-element.88), channel_id=1, source_target_pairs={{0,112},{16,64},{32,80},{48,96},{64,48},{80,0},{96,16},{112,32},{1... | collective-permute-start | bytes 786440 | tf_op jit(solution)/shard_map/ppermute | solution.py:441
  233.2 9.8 %copy-start.9 = (bf16[512,256]{1,0:T(8,128)(2,1)}, bf16[512,256]{1,0:T(8,128)(2,1)S(1)}, u32[]{:S(2)}) copy-start(bf16[512,256]{1,0:T(8,128)(2,1)S(1)} %collective-permute-done.16.refs_5_) | copy-start | bytes 786436
  233.2 9.8 %collective-permute-start.12 = (bf16[256,256]{1,0:T(8,128)(2,1)S(1)}, bf16[256,256]{1,0:T(8,128)(2,1)S(1)}, u32[]{:S(2)}, u32[]{:S(2)}) collective-permute-start(bf16[256,256]{1,0:T(8,128)(2,1)S(1)} %get-tuple-element.89), channel_id=1, source_target_pairs={{0,64},{64,0},{1,65},{65,1},{2,66},{66,2},{3,67},{67,3},{4,68},{68... | collective-permute-start | bytes 393224 | tf_op jit(solution)/shard_map/ppermute | solution.py:411
  (9 other events, 35.4 us)
Sparse Core Ops, SparseCore 0:
  11.6 30.4 all-gather.2
  48.0 27.7 all-gather.4
Sparse Core Ops, SparseCore 1:
  85.8 52.5 reduce-scatter.3
  140.7 29.2 reduce-scatter.7
  173.7 33.4 reduce-scatter.5
